TPU v7x, 32 devices: a whole 2x2x4 slice. The times are simulated.
32 devices in a mesh: level: 2 (over x), row: 8 (over z, core), col: 2 (over y).
Axes of the slice: x: 2, y: 2, z: 4, core: 2. Of those that a mesh axis runs over, the one named last changes fastest.
Arguments:
- noise: bfloat16 [64, 512, 512], P('row', ('level', 'col')), may hold values from -6 to 6
- source: bfloat16 [64, 512, 512], P('row', ('level', 'col')), may hold values from -16 to 16
Outputs:
- fine_pressure: float32 [64, 512, 512], P('row', ('level', 'col'))
- coarse_pressure: float32 [32, 256, 256], P('row', ('level', 'col'))
All inputs are finite; a program needn't handle non-finite values.
Results may differ from a plain program's by a relative error of at most 0.00035.
Values sent between devices are 32-bit elements; how exact they have to be, the bound alone decides.
No kernel may reach another device: no remote copies, remote signals or barrier semaphores. Data moves between devices by JAX's collectives and lax.ppermute only.
A program may use at most 256 MiB of HBM per device.

v0:
```python
import functools
import math

import jax
import jax.numpy as jnp
import numpy as np
from jax import lax
from jax.experimental import pallas as pl
from jax.experimental.pallas import tpu as pltpu
from jax.sharding import PartitionSpec as P

JACOBI_WEIGHT = 2.0 / 3.0
CORRELATION = 0.2
FIELD_SCALE = 0.3
DECAY = (2.0 * math.pi * CORRELATION) ** 2
EVERY = ("row", "level", "col")
PLANE = ("level", "col")
MIB = 1 << 20
SUB, LANE = 8, 128


def two_parts(matrix):
    high = matrix.astype(jnp.bfloat16)
    low = (matrix - high.astype(np.float64)).astype(jnp.bfloat16)
    return high, low


def angles(rows, cols, length):
    return 2.0 * np.pi * (np.outer(rows, cols) % length) / length


def third_modes(devices, js):
    return np.array([[d + devices * j for j in js] for d in range(devices)])


def forward_third(length, devices, js):
    theta = angles(third_modes(devices, js).reshape(-1), np.arange(length), length)
    return np.stack([np.cos(theta), -np.sin(theta)], axis=1).reshape(-1, length)


def inverse_third(length, devices, js):
    modes = third_modes(devices, js).reshape(devices // 2, 2, len(js)).transpose(1, 0, 2)
    theta = 2.0 * np.pi * (modes[..., None] * np.arange(length // 2) % length) / length
    both = np.stack([np.cos(theta), -np.sin(theta)], axis=3)
    return both.reshape(2, -1, length // 2)


def second_modes(length):
    return np.arange(length // 2).reshape(-1, 2).T


def second_table(length):
    theta = second_modes(length)[:, None, :] * np.arange(length // 2)[None, :, None]
    theta = 2.0 * np.pi * (theta % length) / length
    return np.concatenate([np.cos(theta), np.sin(theta)], axis=2)


def forward_first(length):
    theta = angles(np.arange(length), np.arange(length), length)
    cos, sin = np.cos(theta), np.sin(theta)
    return np.block([[cos, sin], [-sin, cos]])


def inverse_first(length):
    theta = angles(np.arange(length), np.arange(length), length)
    cos, sin = np.cos(theta), np.sin(theta)
    cos[:, length // 2] = 0.0
    sin[:, length // 2] = 0.0
    return np.block([[cos, -sin], [sin, cos]])


def inverse_first_coarse(length, rows):
    full = inverse_first(length)
    value = full.reshape(2, rows, length // rows, 2 * length)
    turned = np.concatenate([-full[length:], full[:length]]).reshape(value.shape)
    order = lambda x: x.transpose(1, 0, 2, 3).reshape(2 * length, 2 * length)
    return np.concatenate([order(value), order(turned)])


def second_coarse(length, groups):
    theta = angles(second_modes(length).reshape(-1), np.arange(length), length)
    table = np.concatenate([np.cos(theta), np.sin(theta)])
    span = length // groups
    out = np.zeros((2, length, groups, 2, span))
    for pair in range(2):
        out[pair, :, :, pair, :] = table.reshape(length, groups, span)
    return out.reshape(2 * length, 2 * length)


def third_coarse(length, devices, js):
    modes = third_modes(devices, js).reshape(devices, len(js) // 2, 2)
    theta = 2.0 * np.pi * (modes[..., None] * np.arange(length) % length) / length
    both = np.stack([np.cos(theta), -np.sin(theta)])
    return both.transpose(0, 2, 1, 3, 4).reshape(2 * (len(js) // 2) * devices, 2 * length)


def split(x):
    high = x.astype(jnp.bfloat16)
    return high, (x - high.astype(jnp.float32)).astype(jnp.bfloat16)


def dot(a, b):
    return lax.dot_general(a, b, (((1,), (0,)), ((), ())), preferred_element_type=jnp.float32)


def dot_t(a, b):
    return lax.dot_general(a, b, (((1,), (1,)), ((), ())), preferred_element_type=jnp.float32)


def dot3(a, b):
    (ah, al), (bh, bl) = a, b
    return dot(ah, bh) + (dot(ah, bl) + dot(al, bh))


def load(pairs, sems):
    copies = [pltpu.make_async_copy(a, b, sems.at[i]) for i, (a, b) in enumerate(pairs)]
    for copy in copies:
        copy.start()
    return copies


def send(pairs, sems, first):
    copies = [pltpu.make_async_copy(a, b, sems.at[first + i]) for i, (a, b) in enumerate(pairs)]
    for copy in copies:
        copy.start()
    return copies


def forward_kernel(planes, d_hbm, x_hbm, out_hbm, d, x, out, sems):
    rows = d.shape[0] // 2
    parts = [slice(p * LANE, (p + 2) * LANE) for p in range(0, planes, 2)]
    copies = load([(d_hbm, d)] + [(x_hbm.at[at, :], x.at[at, :]) for at in parts], sems)
    copies[0].wait()
    for i, at in enumerate(parts):
        copies[i + 1].wait()
        value = dot_t(d[...], x[at, :])
        value = value[:rows] + value[rows:]
        for h in range(2):
            out[pl.ds(2 * i + h, rows, stride=SUB), :] = value[:, h * LANE : (h + 1) * LANE]
    for copy in send([(out, out_hbm)], sems, 0):
        copy.wait()


def middle_kernel(sizes, scale, b, *rest):
    (first, second, rows, groups, js, low) = sizes
    count = 12
    away, out_hbm, near, rest = rest[:count], rest[count], rest[count + 1 : 2 * count + 1], rest[2 * count + 1 :]
    out, sems, zh, zl, y, oh, ol, qh, ql = rest
    copies = load(list(zip(away, near)), sems)
    csh, csl, fh, fl, ih, il, ch, cl, ich, icl, cch, ccl = near
    q_count = 2 * js
    half, quarter = second // 2, second // 4
    for q in range(q_count):
        for g in range(groups // 2):
            for r in range(0, rows, 2):
                at = r * groups + g
                near_half = jnp.concatenate([b[at, q], b[at + groups, q]], axis=0)
                at += groups // 2
                far_half = jnp.concatenate([b[at, q], b[at + groups, q]], axis=0)
                at = slice(q * first + r * SUB, q * first + (r + 2) * SUB)
                lanes = slice(g * LANE, (g + 1) * LANE)
                zh[0, at, lanes], zl[0, at, lanes] = split(near_half + far_half)
                zh[1, at, lanes], zl[1, at, lanes] = split(near_half - far_half)
    for copy in copies:
        copy.wait()
    wide = 8 * first
    for top in range(0, q_count * first, wide):
        at = slice(top, top + wide)
        for parity in range(2):
            y[parity, at, :] = dot3(
                (zh[parity, at, :], zl[parity, at, :]), (csh[parity], csl[parity])
            )
    mode0 = lax.broadcasted_iota(jnp.int32, (first, second), 0)
    mode0 = jnp.where(mode0 < first // 2, mode0, mode0 - first).astype(jnp.float32)
    lane = lax.broadcasted_iota(jnp.int32, (first, second), 1)
    mode1 = jnp.where(lane < half, lane, lane - half)
    mode1 = jnp.where(mode1 < quarter, 2 * mode1, 2 * (mode1 - quarter) + 1).astype(jnp.float32)
    base = 1.0 + DECAY * (mode0 * mode0 + mode1 * mode1)
    for j in range(js):
        top = j * 2 * first
        re, im = slice(top, top + first), slice(top + first, top + 2 * first)
        cos, sin = slice(0, quarter), slice(quarter, half)
        whole = lambda part, lanes: jnp.concatenate(
            [y[0, part, lanes], y[1, part, lanes]], axis=1
        )
        rc, rs, ic, isn = whole(re, cos), whole(re, sin), whole(im, cos), whole(im, sin)
        wave = jnp.concatenate(
            [
                jnp.concatenate([rc + isn, rc - isn], axis=1),
                jnp.concatenate([ic - rs, ic + rs], axis=1),
            ],
            axis=0,
        )
        spectrum = dot3((fh[...], fl[...]), split(wave))
        amp = jnp.where(lane == half, 0.0, scale[j, 1] / (base + scale[j, 0]))
        scaled = spectrum * jnp.concatenate([amp, amp], axis=0)
        field = dot3((ih[...], il[...]), split(scaled))
        plus, minus = field[:, :half], field[:, half:]
        even, odd = plus + minus, plus - minus
        odd = jnp.concatenate([-odd[first:], odd[:first]], axis=0)
        at = slice(top, top + 2 * first)
        for parity, lanes in enumerate((cos, sin)):
            operand = jnp.concatenate([even[:, lanes], odd[:, lanes]], axis=1)
            oh[parity, at, :], ol[parity, at, :] = split(operand)
        if j < low:
            keep = first // 4
            kept = [
                scaled[at : at + keep, :]
                for at in (0, first - keep, first, 2 * first - keep)
            ]
            band = jnp.concatenate(kept, axis=0)
            low_lane = lax.broadcasted_iota(jnp.int32, (first, quarter), 1) < quarter // 2
            pieces = []
            for at in (0, half):
                upper = pltpu.roll(band[:, at + quarter : at + half], quarter // 2, 1)
                pieces.append(jnp.where(low_lane, band[:, at : at + quarter], upper))
            band = jnp.concatenate(pieces, axis=1)
            field = dot3((ich[...], icl[...]), split(band))
            value, turned = field[:first], field[first:]
            operand = jnp.concatenate(
                [
                    value[:, :quarter] + value[:, quarter:],
                    turned[:, :quarter] - turned[:, quarter:],
                ],
                axis=1,
            )
            at = slice(j // 2 * first, (j // 2 + 1) * first)
            lanes = slice(j % 2 * half, (j % 2 + 1) * half)
            qh[at, lanes], ql[at, lanes] = split(operand)
    copies = []

    def give(value, start):
        tiles = value.shape[0] // first
        for q in range(tiles):
            for r in range(rows):
                for g in range(groups):
                    at = q * first + r * SUB
                    out[r * groups + g, start + q] = value[
                        at : at + SUB, g * LANE : (g + 1) * LANE
                    ]
        at = slice(start, start + tiles)
        copies.extend(send([(out.at[:, at], out_hbm.at[:, at])], sems, len(copies)))

    give(dot3((qh[...], ql[...]), (cch[...], ccl[...])), q_count)
    for top in range(0, q_count * first, wide):
        at = slice(top, top + wide)
        even, odd = (
            dot3((oh[parity, at, :], ol[parity, at, :]), (ch[parity], cl[parity]))
            for parity in range(2)
        )
        give(jnp.concatenate([even + odd, even - odd], axis=1), top // first)
    for copy in copies:
        copy.wait()


def back_kernel(sizes, b, *rest):
    (devices, q_count, tiles, planes, length) = sizes
    away, outs, near, (lh, ll, mh, ml, sems) = rest[:4], rest[4:8], rest[8:12], rest[12:]
    out, coarse, lo, hi = outs
    copies = load(list(zip(away, near)), sems)
    eh, el, ceh, cel = near
    cells = LANE
    for n in range(planes):
        for parity in range(2):
            rows = jnp.concatenate(
                [
                    b[pl.ds(s * tiles * SUB + n, q_count, stride=SUB), :]
                    for s in range(parity, devices, 2)
                ],
                axis=0,
            )
            at = slice(n * LANE, (n + 1) * LANE)
            lh[parity, at, :], ll[parity, at, :] = split(jnp.transpose(rows))
    halves = tiles - q_count
    coarse_planes = planes // 2
    for n in range(coarse_planes):
        rows = jnp.concatenate(
            [
                b[pl.ds((q_count + h) * SUB + c * coarse_planes + n, devices, stride=tiles * SUB), :]
                for c in range(2)
                for h in range(halves)
            ],
            axis=0,
        )
        high, rest_part = split(jnp.transpose(rows))
        mh[n * LANE : (n + 1) * LANE, :] = high
        ml[n * LANE : (n + 1) * LANE, :] = rest_part
    for copy in copies:
        copy.wait()
    for p in range(0, planes, 2):
        at = slice(p * cells, (p + 2) * cells)
        even, odd = (
            dot3((lh[parity, at, :], ll[parity, at, :]), (eh[parity], el[parity]))
            for parity in range(2)
        )
        value = jnp.exp(jnp.concatenate([even + odd, even - odd], axis=1))
        if p == 0:
            lo[: 2 * cells, :] = value
        if p == planes - 2:
            hi[: 2 * cells, :] = value
        out[at, :] = value
    value = dot3((mh[...], ml[...]), (ceh[...], cel[...]))
    half, fourth, short = cells // 2, cells // 4, length // 2
    for n in range(coarse_planes):
        top = n * cells
        part = value[top : top + half, :short] + value[top + half : top + cells, short:]
        part = jnp.exp(part)
        coarse[n * half : (n + 1) * half, :] = part
        for edge, start in ((lo, 0), (hi, coarse_planes - 2)):
            if start <= n < start + 2:
                top = 2 * cells + (n - start) * fourth
                edge[top : top + fourth, :short] = part[:fourth]
                edge[top : top + fourth, short:] = part[fourth:]


def source_kernel(planes, pairs, x, out, lo, hi, left, right, held, summed):
    cells = x.shape[0] // planes
    length = x.shape[1]
    half, fourth = cells // 2, cells // 4
    held[...] = dot(x[...], pairs[...])
    for n in range(planes // 2):
        top = 2 * n * cells
        for at in range(0, out.shape[1], LANE):
            lanes = slice(at, at + LANE)
            summed[...] = held[top : top + cells, lanes] + held[top + cells : top + 2 * cells, lanes]
            out[n * half : (n + 1) * half, lanes] = (
                summed[pl.ds(0, half, stride=2), :] + summed[pl.ds(1, half, stride=2), :]
            )
    for edge, plane in ((lo, 0), (hi, planes - 1)):
        edge[:cells, :] = x[plane * cells : (plane + 1) * cells, :].astype(jnp.float32)
        at = plane // 2 * half
        edge[cells:, : length // 2] = out[at : at + fourth, :]
        edge[cells:, length // 2 :] = out[at + fourth : at + half, :]
    for edge, row in ((left, 0), (right, cells - 1)):
        edge[...] = jnp.zeros_like(edge)
        for n in range(planes):
            at = n * cells + (row // SUB * SUB)
            edge[n : n + 1, :] = x[at : at + SUB, :].astype(jnp.float32)[row % SUB : row % SUB + 1]
        for n in range(planes // 2):
            at = n * half + row // 2
            edge[SUB + n : SUB + n + 1, : length // 2] = out[at : at + 1, :]


def edge_kernel(kappa, coarse, k_lo, k_hi, first, last):
    planes, cells, _ = kappa.shape
    coarse_planes, half, short = coarse.shape
    fourth = half // 2
    for n in range(planes + 2):
        if n == 0:
            held = k_lo.at[cells : 2 * cells, :]
        elif n == planes + 1:
            held = k_hi.at[:cells, :]
        else:
            held = kappa.at[n - 1]
        first[n] = held[:2, :]
        last[n] = held[cells - 2 :, :]
    for n in range(coarse_planes + 2):
        at = planes + 2 + n
        if 0 < n < coarse_planes + 1:
            top, bottom = coarse[n - 1, :2, :], coarse[n - 1, half - 2 :, :]
        else:
            held, start = (k_lo, 2 * cells + fourth) if n == 0 else (k_hi, 2 * cells)
            top = held[start : start + 2, :short]
            bottom = held[start + fourth - 2 : start + fourth, short:]
        first[at, :, :short] = top
        last[at, :, :short] = bottom
        first[at, :, short:] = jnp.zeros((2, short), jnp.float32)
        last[at, :, short:] = jnp.zeros((2, short), jnp.float32)


def beside(parts, ends):
    lane = lax.broadcasted_iota(jnp.int32, parts[0].shape, 1)
    ahead = [pltpu.roll(x, 1, 1) for x in parts]
    behind = [pltpu.roll(x, LANE - 1, 1) for x in parts]
    sums = []
    for i in range(len(parts)):
        left = jnp.where(lane == 0, ahead[i - 1] if i else ends[0], ahead[i])
        right = jnp.where(
            lane == LANE - 1, behind[i + 1] if i + 1 < len(parts) else ends[1], behind[i]
        )
        sums.append(left + right)
    return sums


def stencil_kernel(
    fine, flags, kappa, k_lo, k_hi, f_lo, f_hi, k_left, k_right, f, f_left, f_right,
    out, ks, fs, us, ws, rs, sems,
):
    planes, cells, length = out.shape
    end = SUB + cells
    pairs = [(kappa, ks.at[2 : planes + 2, SUB:end, :])]

    def place(edge, row, held, plane):
        if fine:
            pairs.append((edge.at[row : row + cells, :], held.at[plane, SUB:end, :]))
            return
        half = cells // 2
        for h in range(2):
            at = SUB + h * half
            pairs.append(
                (
                    edge.at[row : row + half, h * length : (h + 1) * length],
                    held.at[plane, at : at + half, :],
                )
            )

    for i in range(2):
        row = i * cells if fine else 4 * cells + i * cells // 2
        place(k_lo, row, ks, i)
        place(k_hi, row, ks, planes + 2 + i)
    row = 0 if fine else 2 * cells
    place(f_lo, row, fs, 0)
    place(f_hi, row, fs, planes + 1)
    copies = load(pairs, sems)
    at = 0 if fine else SUB
    for p in range(planes):
        fs[p + 1, SUB:end, :] = f[p].astype(jnp.float32)
        fs[p + 1, SUB - 1 : SUB, :] = f_left[at + p : at + p + 1, :length]
        fs[p + 1, end : end + 1, :] = f_right[at + p : at + p + 1, :length]
    at = 0 if fine else 2 * planes + 2
    for p in range(planes + 2):
        ks[p + 1, SUB - 2 : SUB, :] = k_left[at + p, :, :length]
        ks[p + 1, end : end + 2, :] = k_right[at + p, :, :length]
    for copy in copies:
        copy.wait()

    @pl.when(flags[0] == 1)
    def _():
        ks[1] = ks[2]

    @pl.when(flags[1] == 1)
    def _():
        ks[planes + 2] = ks[planes + 1]

    @pl.when(flags[2] == 1)
    def _():
        for p in range(planes + 4):
            ks[p, SUB - 1 : SUB, :] = ks[p, SUB : SUB + 1, :]

    @pl.when(flags[3] == 1)
    def _():
        for p in range(planes + 4):
            ks[p, end : end + 1, :] = ks[p, end - 1 : end, :]

    lanes = [slice(at, at + LANE) for at in range(0, length, LANE)]

    def first(p, carry):
        for top in range(0, cells + 2 * SUB, SUB):
            at = slice(top, top + SUB)
            parts = [ks[p + 1, at, x] for x in lanes]
            for k, both, x in zip(parts, beside(parts, (parts[0], parts[-1])), lanes):
                if top == 0:
                    above = pltpu.roll(k, 1, 0)
                else:
                    above = ks[p + 1, top - 1 : top + SUB - 1, x]
                if top == cells + SUB:
                    below = pltpu.roll(k, SUB - 1, 0)
                else:
                    below = ks[p + 1, top + 1 : top + SUB + 1, x]
                total = (ks[p, at, x] + ks[p + 2, at, x]) + (above + below) + both
                scale = JACOBI_WEIGHT / (6.0 * k + total)
                u = fs[p, at, x] * (2.0 * scale)
                us[p, at, x] = u
                ws[p, at, x] = k * u
                rs[p, at, x] = scale
        return carry

    lax.fori_loop(0, planes + 2, first, 0)

    def second(p, carry):
        for top in range(SUB, end, SUB):
            at = slice(top, top + SUB)
            sums = []
            for held in (us, ws):
                parts = [held[p + 1, at, x] for x in lanes]
                sums.append(
                    [
                        both
                        + (held[p, at, x] + held[p + 2, at, x])
                        + (
                            held[p + 1, top - 1 : top + SUB - 1, x]
                            + held[p + 1, top + 1 : top + SUB + 1, x]
                        )
                        for both, x in zip(beside(parts, (0.0, 0.0)), lanes)
                    ]
                )
            for i, x in enumerate(lanes):
                coupled = ks[p + 2, at, x] * sums[0][i] + sums[1][i]
                out[p, top - SUB : top, x] = (2.0 - JACOBI_WEIGHT) * us[
                    p + 1, at, x
                ] + rs[p + 1, at, x] * coupled
        return carry

    lax.fori_loop(0, planes, second, 0)


SMEM = pl.BlockSpec(memory_space=pltpu.SMEM)
VMEM = pl.BlockSpec(memory_space=pltpu.VMEM)
AWAY = pl.BlockSpec(memory_space=pltpu.HBM)
ANY = pl.BlockSpec(memory_space=pl.ANY)


def call(kernel, outs, operands, scratch, flops, specs, limit):
    many = isinstance(outs, (list, tuple))
    written = outs if many else [outs]
    moved = sum(math.prod(x.shape) * x.dtype.itemsize for x in (*operands, *written))
    operands = [
        pltpu.with_memory_space_constraint(x, pltpu.HBM) if spec is AWAY else x
        for x, spec in zip(operands, specs)
    ]
    out_specs = [VMEM if isinstance(x, jax.ShapeDtypeStruct) else AWAY for x in written]
    return pl.pallas_call(
        kernel,
        out_shape=outs,
        in_specs=specs,
        out_specs=out_specs if many else out_specs[0],
        scratch_shapes=scratch,
        compiler_params=pltpu.CompilerParams(vmem_limit_bytes=limit * MIB),
        cost_estimate=pl.CostEstimate(flops=flops, bytes_accessed=moved, transcendentals=0),
    )(*operands)


def f32(*shape):
    return jax.ShapeDtypeStruct(shape, jnp.float32)


def room(*arrays):
    return [pltpu.VMEM(x.shape, x.dtype) for x in arrays]


def chain(axis):
    up = [(i, i + 1) for i in range(lax.axis_size(axis) - 1)]
    return up, [(j, i) for i, j in up]


def swap(lo, hi, axis):
    up, down = chain(axis)
    return lax.ppermute(hi, axis, up), lax.ppermute(lo, axis, down)


def smooth(fine, flags, kappa, halo, source, edges):
    planes, cells, length = source.shape
    k_lo, k_hi, k_left, k_right = halo
    f_lo, f_hi, f_left, f_right = edges
    ext = cells + 2 * SUB
    wide = pltpu.VMEM((planes + 2, ext, length), jnp.float32)
    return call(
        functools.partial(stencil_kernel, fine),
        f32(planes, cells, length),
        (flags, kappa, k_lo, k_hi, f_lo, f_hi, k_left, k_right, source, f_left, f_right),
        [
            pltpu.VMEM((planes + 4, ext, length), jnp.float32),
            wide, wide, wide, wide,
            pltpu.SemaphoreType.DMA((13,)),
        ],
        60 * kappa.size,
        [SMEM] + [ANY] * 5 + [VMEM] * 5,
        32,
    )


def fused_body(noise, source):
    rows, groups = lax.axis_size("row"), lax.axis_size(PLANE)
    devices = rows * groups
    planes, cells, length = noise.shape
    first, second = planes * rows, cells * groups
    bf16 = jnp.bfloat16
    held = length // 2 // devices
    js = list(range(held))
    low = held // 2
    me = lax.axis_index(EVERY)
    row_at, group_at = lax.axis_index("row"), lax.axis_index(PLANE)
    flags = jnp.stack(
        [row_at == 0, row_at == rows - 1, group_at == 0, group_at == groups - 1]
    ).astype(jnp.int32)
    norm = FIELD_SCALE * (float(first) * float(second) * float(length)) ** (-0.5)
    flat = (planes * cells, length)

    table = np.concatenate(two_parts(forward_third(length, devices, js)))
    shape = (length * SUB, LANE)
    sent = call(
        functools.partial(forward_kernel, planes),
        pltpu.HBM(shape, jnp.float32),
        (table, noise.reshape(flat)),
        room(table)
        + [
            pltpu.VMEM(flat, bf16),
            pltpu.VMEM(shape, jnp.float32),
            pltpu.SemaphoreType.DMA((1 + planes // 2,)),
        ],
        4 * length * length * planes * cells,
        [AWAY] * 2,
        16,
    )
    sent, source = lax.optimization_barrier((sent, source))
    sent = sent.reshape(devices, 2 * held, SUB, LANE)
    arrived = lax.all_to_all(sent, EVERY, split_axis=0, concat_axis=0, tiled=True)

    pairs = np.zeros((length, length // 2), np.float32)
    pairs[np.arange(length), np.arange(length) // 2] = 0.125
    level = f32(cells + cells // 4, length)
    side = f32(2 * SUB, length)
    coarse_source, *edges = call(
        functools.partial(source_kernel, planes),
        [f32(planes * cells // 4, length // 2), level, level, side, side],
        (pairs.astype(bf16), source.reshape(flat)),
        [
            pltpu.VMEM((planes * cells, length // 2), jnp.float32),
            pltpu.VMEM((cells, LANE), jnp.float32),
        ],
        planes * cells * length * length,
        [VMEM] * 2,
        16,
    )
    coarse_source = coarse_source.reshape(planes // 2, cells // 2, length // 2)
    edges = (*swap(*edges[:2], "row"), *swap(*edges[2:], PLANE))
    arrived, edges, coarse_source = lax.optimization_barrier((arrived, edges, coarse_source))

    constants = (
        two_parts(second_table(second))
        + two_parts(forward_first(first))
        + two_parts(inverse_first(first))
        + two_parts(second_table(second).transpose(0, 2, 1))
        + two_parts(inverse_first_coarse(first // 2, rows))
        + two_parts(second_coarse(second // 2, groups))
    )
    tiles = 2 * held + low // 2
    modes = (me + devices * np.array(js)).astype(jnp.float32)
    weight = jnp.where(modes == 0.0, norm, 2.0 * norm).astype(jnp.float32)
    scale = jnp.stack([DECAY * modes * modes, weight], axis=1)
    block = (2, 2 * held * first, second // 2)
    shape = (devices, tiles, SUB, LANE)
    out = call(
        functools.partial(middle_kernel, (first, second, rows, groups, held, low)),
        pltpu.HBM(shape, jnp.float32),
        (scale, arrived, *constants),
        room(*constants)
        + [
            pltpu.VMEM(shape, jnp.float32),
            pltpu.SemaphoreType.DMA((len(constants),)),
            pltpu.VMEM(block, bf16),
            pltpu.VMEM(block, bf16),
            pltpu.VMEM(block, jnp.float32),
            pltpu.VMEM(block, bf16),
            pltpu.VMEM(block, bf16),
            pltpu.VMEM((low // 2 * first, second), bf16),
            pltpu.VMEM((low // 2 * first, second), bf16),
        ],
        6 * 2 * 2 * held * first * second * (second + 2 * first),
        [SMEM, VMEM] + [AWAY] * len(constants),
        32,
    )
    got = lax.all_to_all(out, EVERY, split_axis=0, concat_axis=0, tiled=True)

    constants = two_parts(inverse_third(length, devices, js)) + two_parts(
        third_coarse(length // 2, devices, js[:low])
    )
    edge = f32(2 * cells + cells // 2, length)
    fine, coarse, lo, hi = call(
        functools.partial(back_kernel, (devices, 2 * held, tiles, planes, length)),
        [f32(*flat), f32(planes * cells // 4, length // 2), edge, edge],
        (got.reshape(devices * tiles * SUB, LANE), *constants),
        room(*constants)
        + [pltpu.VMEM((2, planes * cells, devices * held), bf16)] * 2
        + [pltpu.VMEM((planes // 2 * LANE, devices * low), bf16)] * 2
        + [pltpu.SemaphoreType.DMA((4,))],
        6 * planes * cells * length * length,
        [VMEM] + [AWAY] * 4,
        24,
    )
    fine, coarse = fine.reshape(source.shape), coarse.reshape(coarse_source.shape)
    k_lo, k_hi = swap(lo, hi, "row")
    side = f32(planes + planes // 2 + 4, 2, length)
    left, right = call(
        edge_kernel, [side, side], (fine, coarse, k_lo, k_hi), [], fine.size, [VMEM] * 4, 16
    )
    halo = (k_lo, k_hi, *swap(left, right, PLANE))
    fine_pressure = smooth(True, flags, fine, halo, source, edges)
    coarse_pressure = smooth(False, flags, coarse, halo, coarse_source, edges)
    return fine_pressure, coarse_pressure


NEIGHBOUR_STEPS = ((1, 0, 0), (-1, 0, 0), (0, 1, 0), (0, -1, 0), (0, 0, 1), (0, 0, -1))


def padded(x, sides, width):
    for axis, dim in sides:
        peers, length = (lax.axis_size(axis), x.shape[dim])
        up = [(i, (i + 1) % peers) for i in range(peers - 1)]
        down = [(j, i) for i, j in up]
        last = lax.slice_in_dim(x, length - width, length, axis=dim)
        leading = lax.slice_in_dim(x, 0, width, axis=dim)
        before = lax.ppermute(last, axis, up)
        after = lax.ppermute(leading, axis, down)
        x = jnp.concatenate([before, x, after], axis=dim)
    return x


def signed_modes(index, length):
    return jnp.where(index < length // 2, index, index - length).astype(jnp.float32)


def amplitude(first_modes, second_modes, third_modes, first_edge, second_edge, third_edge):
    squared = first_modes * first_modes + second_modes * second_modes + third_modes * third_modes
    value = FIELD_SCALE / (1.0 + (2.0 * math.pi * CORRELATION) ** 2 * squared)
    edge = (
        (jnp.abs(first_modes) == first_edge)
        | (jnp.abs(second_modes) == second_edge)
        | (jnp.abs(third_modes) == third_edge)
    )
    return jnp.where(edge, 0.0, value)


def phase_table(count_rows, count_cols, modulus, sign):
    left_index = jnp.arange(count_rows, dtype=jnp.int32)[:, None]
    right_index = jnp.arange(count_cols, dtype=jnp.int32)[None, :]
    angle = 2.0 * math.pi / modulus * (left_index * right_index % modulus).astype(jnp.float32)
    return (jnp.cos(angle), sign * jnp.sin(angle))


def split_length(length):
    outer_len = 2 ** ((length.bit_length() - 1) // 2)
    return (outer_len, length // outer_len)


def real_form(form, left_value, right_value):
    return jnp.einsum(form, left_value, right_value, precision=lax.Precision.HIGHEST)


def complex_form(form, left_real, left_imag, right_real, right_imag):
    real_part = real_form(form, left_real, right_real) - real_form(form, left_imag, right_imag)
    imag_part = real_form(form, left_real, right_imag) + real_form(form, left_imag, right_real)
    return (real_part, imag_part)


def merge_pair(values, out_form, first_letter):
    merge_at = out_form.index(first_letter)
    out_dims = list(values.shape)
    merged = (
        out_dims[:merge_at]
        + [out_dims[merge_at] * out_dims[merge_at + 1]]
        + out_dims[merge_at + 2 :]
    )
    return values.reshape(merged)


def forward_axis(real_part, imag_part, lead_form, out_form, kept_modes):
    length = real_part.shape[-1]
    outer_len, inner_len = split_length(length)
    split_shape = real_part.shape[:-1] + (outer_len, inner_len)
    outer_real, outer_imag = phase_table(outer_len, outer_len, outer_len, -1.0)
    twist_real, twist_imag = phase_table(outer_len, inner_len, length, -1.0)
    inner_real, inner_imag = phase_table(inner_len, kept_modes // outer_len, inner_len, -1.0)
    first_form = lead_form + "ab,ai->" + lead_form + "ib"
    split_real = real_part.reshape(split_shape)
    if imag_part is None:
        section_real = real_form(first_form, split_real, outer_real)
        section_imag = real_form(first_form, split_real, outer_imag)
    else:
        section_real, section_imag = complex_form(
            first_form, split_real, imag_part.reshape(split_shape), outer_real, outer_imag
        )
    turned_real = section_real * twist_real - section_imag * twist_imag
    turned_imag = section_real * twist_imag + section_imag * twist_real
    result_real, result_imag = complex_form(
        lead_form + "ib,bj->" + out_form, turned_real, turned_imag, inner_real, inner_imag
    )
    return (merge_pair(result_real, out_form, "j"), merge_pair(result_imag, out_form, "j"))


def inverse_axis(real_part, imag_part, length, lead_form, out_form, real_only):
    kept_modes = real_part.shape[-1]
    outer_len, inner_len = split_length(length)
    split_shape = real_part.shape[:-1] + (kept_modes // outer_len, outer_len)
    inner_real, inner_imag = phase_table(kept_modes // outer_len, inner_len, inner_len, 1.0)
    twist_real, twist_imag = phase_table(outer_len, inner_len, length, 1.0)
    outer_real, outer_imag = phase_table(outer_len, outer_len, outer_len, 1.0)
    section_real, section_imag = complex_form(
        lead_form + "ji,jb->" + lead_form + "ib",
        real_part.reshape(split_shape),
        imag_part.reshape(split_shape),
        inner_real,
        inner_imag,
    )
    turned_real = section_real * twist_real - section_imag * twist_imag
    turned_imag = section_real * twist_imag + section_imag * twist_real
    second_form = lead_form + "ib,ia->" + out_form
    if real_only:
        result = real_form(second_form, turned_real, outer_real) - real_form(
            second_form, turned_imag, outer_imag
        )
        return merge_pair(result, out_form, "a")
    result_real, result_imag = complex_form(
        second_form, turned_real, turned_imag, outer_real, outer_imag
    )
    return (merge_pair(result_real, out_form, "a"), merge_pair(result_imag, out_form, "a"))


def low_band(values, half_coarse, fine_len):
    return jnp.concatenate(
        [values[:, :, :half_coarse], values[:, :, fine_len - half_coarse :]], axis=2
    )


def window(values, margin, offset):
    return values[
        margin + offset[0] : values.shape[0] - margin + offset[0],
        margin + offset[1] : values.shape[1] - margin + offset[1],
        margin + offset[2] : values.shape[2] - margin + offset[2],
    ]


def face_weight(center, beside):
    return jnp.where(beside > 0.0, 0.5 * (center + beside), center)


def smooth_twice(kappa, source):
    no_shift = (0, 0, 0)
    center = window(kappa, 1, no_shift)
    faces = [face_weight(center, window(kappa, 1, offset)) for offset in NEIGHBOUR_STEPS]
    diagonal = faces[0] + faces[1] + faces[2] + faces[3] + faces[4] + faces[5]
    guarded = jnp.where(center > 0.0, diagonal, 1.0)
    first_sweep = JACOBI_WEIGHT * window(source, 1, no_shift) / guarded
    inner_first = window(first_sweep, 1, no_shift)
    inner_diagonal = window(diagonal, 1, no_shift)
    coupled = jnp.zeros_like(inner_first)
    for face_value, offset in zip(faces, NEIGHBOUR_STEPS):
        coupled = coupled + window(face_value, 1, no_shift) * window(first_sweep, 1, offset)
    residual = window(source, 2, no_shift) - inner_diagonal * inner_first + coupled
    return inner_first + JACOBI_WEIGHT * residual / inner_diagonal


def pad_depth(values):
    return jnp.pad(values, ((0, 0), (0, 0), (2, 2)))


def plain_body(noise, source):
    row_at = lax.axis_index("row")
    group_at = lax.axis_index(("level", "col"))
    fine_field = noise.astype(jnp.float32)
    fine_len = fine_field.shape[-1]
    coarse_len = fine_len // 2
    half_coarse = coarse_len // 2
    kept_modes = fine_len // 2
    real_part, imag_part = forward_axis(fine_field, None, "pq", "pjiq", kept_modes)
    real_part, imag_part = (
        lax.all_to_all(real_part, ("level", "col"), split_axis=1, concat_axis=2, tiled=True),
        lax.all_to_all(imag_part, ("level", "col"), split_axis=1, concat_axis=2, tiled=True),
    )
    real_part, imag_part = forward_axis(real_part, imag_part, "pq", "jiqp", fine_len)
    real_part, imag_part = (
        lax.all_to_all(real_part, "row", split_axis=0, concat_axis=2, tiled=True),
        lax.all_to_all(imag_part, "row", split_axis=0, concat_axis=2, tiled=True),
    )
    slab_len = real_part.shape[-1]
    coarse_slab = slab_len // 2
    half_slab = coarse_slab // 2
    real_part, imag_part = forward_axis(real_part, imag_part, "pq", "pqji", slab_len)
    second_count = real_part.shape[0]
    third_count = real_part.shape[1]
    wave_second = signed_modes(
        row_at * second_count + jnp.arange(second_count, dtype=jnp.int32), fine_len
    )[:, None, None]
    third_index = group_at * third_count + jnp.arange(third_count, dtype=jnp.int32)
    wave_third = signed_modes(third_index, fine_len)[None, :, None]
    spread = 2.0
    mirror_weight = jnp.where(third_index == 0, 1.0, spread).astype(jnp.float32)[None, :, None]
    norm_factor = (float(slab_len) * float(fine_len) * float(fine_len)) ** (-0.5)
    wave_first = signed_modes(jnp.arange(slab_len, dtype=jnp.int32), slab_len)[None, None, :]
    fine_scale = (
        amplitude(
            wave_second, wave_third, wave_first, fine_len / 2.0, fine_len / 2.0, slab_len / 2.0
        )
        * mirror_weight
        * norm_factor
    )
    coarse_first = signed_modes(jnp.arange(coarse_slab, dtype=jnp.int32), coarse_slab)[
        None, None, :
    ]
    coarse_scale = (
        amplitude(
            wave_second,
            wave_third,
            coarse_first,
            coarse_len / 2.0,
            coarse_len / 2.0,
            coarse_slab / 2.0,
        )
        * mirror_weight
        * norm_factor
    )
    coarse_real = low_band(real_part, half_slab, slab_len) * coarse_scale
    coarse_imag = low_band(imag_part, half_slab, slab_len) * coarse_scale
    fine_real, fine_imag = inverse_axis(
        real_part * fine_scale, imag_part * fine_scale, slab_len, "pq", "abqp", False
    )
    coarse_real, coarse_imag = inverse_axis(
        coarse_real, coarse_imag, coarse_slab, "pq", "abqp", False
    )
    fine_real, fine_imag, coarse_real, coarse_imag = (
        lax.all_to_all(fine_real, "row", split_axis=0, concat_axis=2, tiled=True),
        lax.all_to_all(fine_imag, "row", split_axis=0, concat_axis=2, tiled=True),
        lax.all_to_all(coarse_real, "row", split_axis=0, concat_axis=2, tiled=True),
        lax.all_to_all(coarse_imag, "row", split_axis=0, concat_axis=2, tiled=True),
    )
    coarse_real = low_band(coarse_real, half_coarse, fine_len)
    coarse_imag = low_band(coarse_imag, half_coarse, fine_len)
    fine_real, fine_imag = inverse_axis(fine_real, fine_imag, fine_len, "pq", "pabq", False)
    coarse_real, coarse_imag = inverse_axis(
        coarse_real, coarse_imag, coarse_len, "pq", "pabq", False
    )
    fine_real, fine_imag, coarse_real, coarse_imag = (
        lax.all_to_all(fine_real, ("level", "col"), split_axis=1, concat_axis=2, tiled=True),
        lax.all_to_all(fine_imag, ("level", "col"), split_axis=1, concat_axis=2, tiled=True),
        lax.all_to_all(coarse_real, ("level", "col"), split_axis=1, concat_axis=2, tiled=True),
        lax.all_to_all(coarse_imag, ("level", "col"), split_axis=1, concat_axis=2, tiled=True),
    )
    coarse_real = coarse_real[:, :, :half_coarse]
    coarse_imag = coarse_imag[:, :, :half_coarse]
    fine_log = inverse_axis(fine_real, fine_imag, fine_len, "pq", "pqab", True)
    coarse_log = inverse_axis(coarse_real, coarse_imag, coarse_len, "pq", "pqab", True)
    fine_kappa = jnp.exp(fine_log)
    coarse_kappa = jnp.exp(coarse_log)
    fine_source = source.astype(jnp.float32)
    coarse_rows = coarse_log.shape[0]
    coarse_cols = coarse_log.shape[1]
    coarse_source = fine_source.reshape(coarse_rows, 2, coarse_cols, 2, coarse_len, 2).mean(
        axis=(1, 3, 5)
    )
    fine_kappa, fine_source, coarse_kappa, coarse_source = (
        padded(fine_kappa, (("row", 0), (("level", "col"), 1)), 2),
        padded(fine_source, (("row", 0), (("level", "col"), 1)), 2),
        padded(coarse_kappa, (("row", 0), (("level", "col"), 1)), 2),
        padded(coarse_source, (("row", 0), (("level", "col"), 1)), 2),
    )
    fine_pressure = smooth_twice(pad_depth(fine_kappa), pad_depth(fine_source))
    coarse_pressure = smooth_twice(pad_depth(coarse_kappa), pad_depth(coarse_source))
    return (fine_pressure, coarse_pressure)


def body(noise, source):
    planes, cells, length = noise.shape
    devices = lax.axis_size(EVERY)
    held = length // 2 // devices
    if planes == SUB and cells == LANE and held % 4 == 0 and held > 0:
        return fused_body(noise, source)
    return plain_body(noise, source)


def solution(mesh):
    return jax.shard_map(
        body,
        mesh=mesh,
        in_specs=(P("row", ("level", "col"), None), P("row", ("level", "col"), None)),
        out_specs=(P("row", ("level", "col"), None), P("row", ("level", "col"), None)),
        check_vma=False,
    )
```

profile of v0, /device:TPU:1, one launch (start us, length us, event | category | flops | bytes accessed | tf_op | source)
XLA Modules:
  0.0 170.7 jit_solution(14479304291889807326)
XLA Ops:
  0.6 5.5 %shard_map.212 = f32[4096,128]{1,0:T(8,128)} custom-call(bf16[1024,512]{1,0:T(8,128)(2,1)} %constant.69.clone.d_hbm, bf16[1024,512]{1,0:T(8,128)(2,1)} %bitcast.23), custom_call_target="tpu_custom_call" | custom-call | flops 1073741824 | bytes 4194304 | tf_op jit(solution)/shard_map/pallas_call | solution.py:512
  6.2 7.1 %all-to-all-start = ((f32[32,16,8,128]{3,2,1,0:T(8,128)}), f32[32,16,8,128]{3,2,1,0:T(8,128)S(1)}, u32[]{:S(2)}, u32[]{:S(2)}) async-start(f32[32,16,8,128]{3,2,1,0:T(8,128)} %bitcast.22), calls=%async_computation | async-start | bytes 4194304 | tf_op jit(solution)/shard_map/all_to_all | solution.py:597
  13.3 1.3 shard_map.213
  14.6 0.7 copy-done.8
  15.3 3.5 %collective-permute-start = (f32[160,512]{1,0:T(8,128)}, f32[160,512]{1,0:T(8,128)S(1)}, u32[]{:S(2)}, u32[]{:S(2)}) collective-permute-start(f32[160,512]{1,0:T(8,128)} %get-tuple-element.23), channel_id=1, source_target_pairs={{0,2},{2,4},{4,6},{6,8},{8,10},{10,12},{12,14},{1,3},{3,5},{5,7},{... | collective-permute-start | bytes 983048 | tf_op jit(solution)/shard_map/ppermute | solution.py:538
  18.8 1.9 %collective-permute-start.1 = (f32[160,512]{1,0:T(8,128)}, f32[160,512]{1,0:T(8,128)S(1)}, u32[]{:S(2)}, u32[]{:S(2)}) collective-permute-start(f32[160,512]{1,0:T(8,128)} %get-tuple-element.24), channel_id=1, source_target_pairs={{2,0},{4,2},{6,4},{8,6},{10,8},{12,10},{14,12},{3,1},{5,3},{7,5},{... | collective-permute-start | bytes 983048 | tf_op jit(solution)/shard_map/ppermute | solution.py:538
  20.8 3.1 %collective-permute-start.2 = (f32[16,512]{1,0:T(8,128)S(1)}, f32[16,512]{1,0:T(8,128)S(1)}, u32[]{:S(2)}, u32[]{:S(2)}) collective-permute-start(f32[16,512]{1,0:T(8,128)S(1)} %get-tuple-element.25), channel_id=1, source_target_pairs={{0,1},{1,16},{16,17},{2,3},{3,18},{18,19},{4,5},{5,20},{20,21},{6,... | collective-permute-start | bytes 98312 | tf_op jit(solution)/shard_map/ppermute | solution.py:538
  23.9 1.3 collective-permute-start.3
  25.3 4.0 %collective-permute-done.3.f_right = f32[16,512]{1,0:T(8,128)S(1)} collective-permute-done((f32[16,512]{1,0:T(8,128)S(1)}, f32[16,512]{1,0:T(8,128)S(1)}, u32[]{:S(2)}, u32[]{:S(2)}) %collective-permute-start.3) | collective-permute-done | bytes 32800 | tf_op jit(solution)/shard_map/ppermute | solution.py:538
  29.3 22.1 %collective-permute-done.f_lo = f32[160,512]{1,0:T(8,128)S(1)} collective-permute-done((f32[160,512]{1,0:T(8,128)}, f32[160,512]{1,0:T(8,128)S(1)}, u32[]{:S(2)}, u32[]{:S(2)}) %collective-permute-start) | collective-permute-done | bytes 327712 | tf_op jit(solution)/shard_map/ppermute | solution.py:538
  51.4 10.0 %all-to-all-done.b = f32[32,16,8,128]{3,2,1,0:T(8,128)S(1)} async-done(((f32[32,16,8,128]{3,2,1,0:T(8,128)}), f32[32,16,8,128]{3,2,1,0:T(8,128)S(1)}, u32[]{:S(2)}, u32[]{:S(2)}) %all-to-all-start) | async-done | bytes 2097184 | tf_op jit(solution)/shard_map/all_to_all | solution.py:597
  61.4 8.4 %shard_map.214 = f32[32,18,8,128]{3,2,1,0:T(8,128)} custom-call(f32[8,2]{1,0:T(8,128)S(1)} %copy.25.scale, f32[32,16,8,128]{3,2,1,0:T(8,128)S(1)} %all-to-all-done.b, bf16[2,256,256]{2,1,0:T(8,128)(2,1)} %constant.72.clone.rest_0_, bf16[2,256,256]{2,1,0:T(8,128)(2,1)} %constant.73.clone.rest_1_, bf16[128,128]{1,0:T(8,128)(2,1)} %constant.74.clone.rest_2_, ...), custom_call_target="tpu_custom_call" | custom-call | flops 4026531840 | bytes 6717504 | tf_op jit(solution)/shard_map/pallas_call | solution.py:512
  69.9 61.9 %all_to_all.10 = f32[32,18,8,128]{3,2,1,0:T(8,128)S(1)} all-to-all(f32[32,18,8,128]{3,2,1,0:T(8,128)} %shard_map.214), channel_id=1, replica_groups=mesh['level'=2,'row'=8,'col'=2] {'row','level','col'}, dimensions={0} | all-to-all | bytes 4718592 | tf_op jit(solution)/shard_map/all_to_all | solution.py:653
  131.7 4.2 %shard_map.215 = (f32[1024,512]{1,0:T(8,128)S(1)}, f32[256,256]{1,0:T(8,128)S(1)}, f32[320,512]{1,0:T(8,128)}, f32[320,512]{1,0:T(8,128)}) custom-call(f32[4608,128]{1,0:T(8,128)S(1)} %bitcast.18, bf16[2,256,256]{2,1,0:T(8,128)(2,1)} %constant.84.clone.rest_0_, bf16[2,256,256]{2,1,0:T(8,128)(2,1)} %constant.85.clone.rest_1_, ...), custom_call_target="tpu_custom_call" | custom-call | flops 1610612736 | bytes 6815744 | tf_op jit(solution)/shard_map/pallas_call | solution.py:512
  136.6 3.5 %collective-permute-start.4 = (f32[320,512]{1,0:T(8,128)}, f32[320,512]{1,0:T(8,128)S(1)}, u32[]{:S(2)}, u32[]{:S(2)}) collective-permute-start(f32[320,512]{1,0:T(8,128)} %get-tuple-element.30), channel_id=1, source_target_pairs={{0,2},{2,4},{4,6},{6,8},{8,10},{10,12},{12,14},{1,3},{3,5},{5,7},{... | collective-permute-start | bytes 1966088 | tf_op jit(solution)/shard_map/ppermute | solution.py:538
  140.1 1.9 %collective-permute-start.5 = (f32[320,512]{1,0:T(8,128)}, f32[320,512]{1,0:T(8,128)S(1)}, u32[]{:S(2)}, u32[]{:S(2)}) collective-permute-start(f32[320,512]{1,0:T(8,128)} %get-tuple-element.31), channel_id=1, source_target_pairs={{2,0},{4,2},{6,4},{8,6},{10,8},{12,10},{14,12},{3,1},{5,3},{7,5},{... | collective-permute-start | bytes 1966088 | tf_op jit(solution)/shard_map/ppermute | solution.py:538
  142.1 5.8 %collective-permute-done.4.k_lo = f32[320,512]{1,0:T(8,128)S(1)} collective-permute-done((f32[320,512]{1,0:T(8,128)}, f32[320,512]{1,0:T(8,128)S(1)}, u32[]{:S(2)}, u32[]{:S(2)}) %collective-permute-start.4) | collective-permute-done | bytes 655392 | tf_op jit(solution)/shard_map/ppermute | solution.py:538
  147.9 4.3 %collective-permute-done.5.k_hi = f32[320,512]{1,0:T(8,128)S(1)} collective-permute-done((f32[320,512]{1,0:T(8,128)}, f32[320,512]{1,0:T(8,128)S(1)}, u32[]{:S(2)}, u32[]{:S(2)}) %collective-permute-start.5) | collective-permute-done | bytes 655392 | tf_op jit(solution)/shard_map/ppermute | solution.py:538
  152.2 0.9 copy-done.7
  153.2 1.9 %collective-permute-start.6 = (f32[16,2,512]{2,1,0:T(2,128)S(1)}, f32[16,2,512]{2,1,0:T(2,128)S(1)}, u32[]{:S(2)}, u32[]{:S(2)}) collective-permute-start(f32[16,2,512]{2,1,0:T(2,128)S(1)} %get-tuple-element.35), channel_id=1, source_target_pairs={{0,1},{1,16},{16,17},{2,3},{3,18},{18,19},{4,5},{5,20},{20,21},{6,... | collective-permute-start | bytes 196616 | tf_op jit(solution)/shard_map/ppermute | solution.py:538
  155.1 1.3 collective-permute-start.7
  156.5 3.6 %collective-permute-done.7.k_right = f32[16,2,512]{2,1,0:T(2,128)S(1)} collective-permute-done((f32[16,2,512]{2,1,0:T(2,128)S(1)}, f32[16,2,512]{2,1,0:T(2,128)S(1)}, u32[]{:S(2)}, u32[]{:S(2)}) %collective-permute-start.7) | collective-permute-done | bytes 65568 | tf_op jit(solution)/shard_map/ppermute | solution.py:538
  160.1 7.6 %shard_map.217 = f32[8,128,512]{2,1,0:T(8,128)} custom-call(s32[4]{0:T(128)S(1)} %add_convert_fusion.flags, f32[8,128,512]{2,1,0:T(8,128)S(1)} %bitcast.16, f32[320,512]{1,0:T(8,128)S(1)} %collective-permute-done.4.k_lo, f32[320,512]{1,0:T(8,128)S(1)} %collective-permute-done.5.k_hi, f32[160,512]{1,0:T(8,128)S(1)} %copy-done.3, f32[160,512]{1,0:T(8,128)S(1)} %copy-done.5, ...), custom_call_target="tpu_custom_call" | custom-call | flops 31457280 | bytes 7405584 | tf_op jit(solution)/shard_map/pallas_call | solution.py:512
  167.8 2.9 %shard_map.218 = f32[4,64,256]{2,1,0:T(8,128)} custom-call(s32[4]{0:T(128)S(1)} %add_convert_fusion.flags, f32[4,64,256]{2,1,0:T(8,128)S(1)} %bitcast.20, f32[320,512]{1,0:T(8,128)S(1)} %collective-permute-done.4.k_lo, f32[320,512]{1,0:T(8,128)S(1)} %collective-permute-done.5.k_hi, f32[160,512]{1,0:T(8,128)S(1)} %copy-done.3, f32[160,512]{1,0:T(8,128)S(1)} %copy-done.5, ...), custom_call_target="tpu_custom_call" | custom-call | flops 3932160 | bytes 2949136 | tf_op jit(solution)/shard_map/pallas_call | solution.py:512
  (28 shorter events, 1.0 us)
Async XLA Ops:
  6.2 7.1 %copy-start = (bf16[8,128,512]{2,1,0:T(8,128)(2,1)S(1)}, bf16[8,128,512]{2,1,0:T(8,128)(2,1)}, u32[]{:S(2)}) copy-start(bf16[8,128,512]{2,1,0:T(8,128)(2,1)} %f) | copy-start | bytes 3145732
  6.2 7.1 %copy-start.10 = (bf16[512,256]{1,0:T(8,128)(2,1)S(1)}, bf16[512,256]{1,0:T(8,128)(2,1)}, u32[]{:S(2)}) copy-start(bf16[512,256]{1,0:T(8,128)(2,1)} %constant.70.clone.pairs) | copy-start | bytes 786436
  6.2 55.2 %all-to-all-start = ((f32[32,16,8,128]{3,2,1,0:T(8,128)}), f32[32,16,8,128]{3,2,1,0:T(8,128)S(1)}, u32[]{:S(2)}, u32[]{:S(2)}) async-start(f32[32,16,8,128]{3,2,1,0:T(8,128)} %bitcast.22), calls=%async_computation | async-start | bytes 4194304 | tf_op jit(solution)/shard_map/all_to_all | solution.py:597
  14.6 0.7 copy-start.8
  15.3 36.1 %collective-permute-start = (f32[160,512]{1,0:T(8,128)}, f32[160,512]{1,0:T(8,128)S(1)}, u32[]{:S(2)}, u32[]{:S(2)}) collective-permute-start(f32[160,512]{1,0:T(8,128)} %get-tuple-element.23), channel_id=1, source_target_pairs={{0,2},{2,4},{4,6},{6,8},{8,10},{10,12},{12,14},{1,3},{3,5},{5,7},{... | collective-permute-start | bytes 983048 | tf_op jit(solution)/shard_map/ppermute | solution.py:538
  18.8 32.6 %collective-permute-start.1 = (f32[160,512]{1,0:T(8,128)}, f32[160,512]{1,0:T(8,128)S(1)}, u32[]{:S(2)}, u32[]{:S(2)}) collective-permute-start(f32[160,512]{1,0:T(8,128)} %get-tuple-element.24), channel_id=1, source_target_pairs={{2,0},{4,2},{6,4},{8,6},{10,8},{12,10},{14,12},{3,1},{5,3},{7,5},{... | collective-permute-start | bytes 983048 | tf_op jit(solution)/shard_map/ppermute | solution.py:538
  20.8 4.5 %collective-permute-start.2 = (f32[16,512]{1,0:T(8,128)S(1)}, f32[16,512]{1,0:T(8,128)S(1)}, u32[]{:S(2)}, u32[]{:S(2)}) collective-permute-start(f32[16,512]{1,0:T(8,128)S(1)} %get-tuple-element.25), channel_id=1, source_target_pairs={{0,1},{1,16},{16,17},{2,3},{3,18},{18,19},{4,5},{5,20},{20,21},{6,... | collective-permute-start | bytes 98312 | tf_op jit(solution)/shard_map/ppermute | solution.py:538
  23.9 5.5 %collective-permute-start.3 = (f32[16,512]{1,0:T(8,128)S(1)}, f32[16,512]{1,0:T(8,128)S(1)}, u32[]{:S(2)}, u32[]{:S(2)}) collective-permute-start(f32[16,512]{1,0:T(8,128)S(1)} %get-tuple-element.26), channel_id=1, source_target_pairs={{1,0},{16,1},{17,16},{3,2},{18,3},{19,18},{5,4},{20,5},{21,20},{7,... | collective-permute-start | bytes 98312 | tf_op jit(solution)/shard_map/ppermute | solution.py:538
  51.4 18.4 %copy-start.2 = (f32[160,512]{1,0:T(8,128)}, f32[160,512]{1,0:T(8,128)S(1)}, u32[]{:S(2)}) copy-start(f32[160,512]{1,0:T(8,128)S(1)} %collective-permute-done.f_lo) | copy-start | bytes 983044
  51.4 18.4 %copy-start.4 = (f32[160,512]{1,0:T(8,128)}, f32[160,512]{1,0:T(8,128)S(1)}, u32[]{:S(2)}) copy-start(f32[160,512]{1,0:T(8,128)S(1)} %collective-permute-done.1.f_hi) | copy-start | bytes 983044
  135.9 0.7 copy-start.6
  136.6 11.3 %collective-permute-start.4 = (f32[320,512]{1,0:T(8,128)}, f32[320,512]{1,0:T(8,128)S(1)}, u32[]{:S(2)}, u32[]{:S(2)}) collective-permute-start(f32[320,512]{1,0:T(8,128)} %get-tuple-element.30), channel_id=1, source_target_pairs={{0,2},{2,4},{4,6},{6,8},{8,10},{10,12},{12,14},{1,3},{3,5},{5,7},{... | collective-permute-start | bytes 1966088 | tf_op jit(solution)/shard_map/ppermute | solution.py:538
  140.1 12.1 %collective-permute-start.5 = (f32[320,512]{1,0:T(8,128)}, f32[320,512]{1,0:T(8,128)S(1)}, u32[]{:S(2)}, u32[]{:S(2)}) collective-permute-start(f32[320,512]{1,0:T(8,128)} %get-tuple-element.31), channel_id=1, source_target_pairs={{2,0},{4,2},{6,4},{8,6},{10,8},{12,10},{14,12},{3,1},{5,3},{7,5},{... | collective-permute-start | bytes 1966088 | tf_op jit(solution)/shard_map/ppermute | solution.py:538
  142.1 18.1 %copy-start.1 = (bf16[8,128,512]{2,1,0:T(8,128)(2,1)S(1)}, bf16[8,128,512]{2,1,0:T(8,128)(2,1)}, u32[]{:S(2)}) copy-start(bf16[8,128,512]{2,1,0:T(8,128)(2,1)} %f) | copy-start | bytes 3145732
  142.1 18.1 %copy-start.3 = (f32[160,512]{1,0:T(8,128)S(1)}, f32[160,512]{1,0:T(8,128)}, u32[]{:S(2)}) copy-start(f32[160,512]{1,0:T(8,128)} %copy-done.2) | copy-start | bytes 983044
  142.1 18.0 %copy-start.5 = (f32[160,512]{1,0:T(8,128)S(1)}, f32[160,512]{1,0:T(8,128)}, u32[]{:S(2)}) copy-start(f32[160,512]{1,0:T(8,128)} %copy-done.4) | copy-start | bytes 983044
  152.2 1.0 copy-start.7
  153.2 3.3 %collective-permute-start.6 = (f32[16,2,512]{2,1,0:T(2,128)S(1)}, f32[16,2,512]{2,1,0:T(2,128)S(1)}, u32[]{:S(2)}, u32[]{:S(2)}) collective-permute-start(f32[16,2,512]{2,1,0:T(2,128)S(1)} %get-tuple-element.35), channel_id=1, source_target_pairs={{0,1},{1,16},{16,17},{2,3},{3,18},{18,19},{4,5},{5,20},{20,21},{6,... | collective-permute-start | bytes 196616 | tf_op jit(solution)/shard_map/ppermute | solution.py:538
  155.1 5.0 %collective-permute-start.7 = (f32[16,2,512]{2,1,0:T(2,128)S(1)}, f32[16,2,512]{2,1,0:T(2,128)S(1)}, u32[]{:S(2)}, u32[]{:S(2)}) collective-permute-start(f32[16,2,512]{2,1,0:T(2,128)S(1)} %get-tuple-element.36), channel_id=1, source_target_pairs={{1,0},{16,1},{17,16},{3,2},{18,3},{19,18},{5,4},{20,5},{21,20},{7,... | collective-permute-start | bytes 196616 | tf_op jit(solution)/shard_map/ppermute | solution.py:538
  156.5 11.3 %copy-start.9 = (f32[256,256]{1,0:T(8,128)S(1)}, f32[256,256]{1,0:T(8,128)}, u32[]{:S(2)}) copy-start(f32[256,256]{1,0:T(8,128)} %copy-done.8) | copy-start | bytes 786436
where the time goes:
time: 171 us
  blocking collectives  61.9 us (36%)
  waiting for transfers between devices  49.9 us (29%)
  Pallas kernels  30 us (18%)
  starting transfers between devices  25.5 us (15%)
  local copies, waits for them, and re-layouts  2.47 us (1%)
    all_to_all x1, blocking collectives, fused_body(): got = lax.all_to_all(out, EVERY, split_axis=0, concat_axis=0, tiled=True)  61.9 us
    ppermute x8, waiting for transfers between devices, swap(): return (lax.ppermute(hi, axis, up), lax.ppermute(lo, axis, down))  39.9 us
    pallas_call x7, Pallas kernels, call(): pl.pallas_call(kernel, out_shape=outs, in_specs=specs, out_specs=out_spec...  30 us
    ppermute x8, starting transfers between devices, swap(): return (lax.ppermute(hi, axis, up), lax.ppermute(lo, axis, down))  18.4 us
    all_to_all x1, waiting for transfers between devices, fused_body(): lax.all_to_all(sent, EVERY, split_axis=0, concat_axis=0, tiled=True)  9.98 us
    all_to_all x1, starting transfers between devices, fused_body(): lax.all_to_all(sent, EVERY, split_axis=0, concat_axis=0, tiled=True)  7.1 us
  transfers between devices with their start and end apart: 9, of which 6 were waited for; matrix products, arithmetic and copies ran while one was open for 0% of the time, Pallas kernels for 1%

commit v1 on v0

--- a/solution.py
+++ b/solution.py
@@ -17,6 +17,7 @@
 PLANE = ("level", "col")
 MIB = 1 << 20
 SUB, LANE = 8, 128
+HALO = 4
 
 
 def two_parts(matrix):
@@ -92,6 +93,12 @@
     theta = 2.0 * np.pi * (modes[..., None] * np.arange(length) % length) / length
     both = np.stack([np.cos(theta), -np.sin(theta)])
     return both.transpose(0, 2, 1, 3, 4).reshape(2 * (len(js) // 2) * devices, 2 * length)
+
+
+def third_coarse_halo(length, devices, js):
+    modes = np.repeat(third_modes(devices, js).reshape(-1), HALO)
+    theta = angles(modes, np.arange(length), length)
+    return np.concatenate([np.cos(theta), -np.sin(theta)], axis=1)
 
 
 def split(x):
@@ -228,6 +235,12 @@
             lanes = slice(j % 2 * half, (j % 2 + 1) * half)
             qh[at, lanes], ql[at, lanes] = split(operand)
     copies = []
+    lane = lax.broadcasted_iota(jnp.int32, (SUB, LANE), 1)
+    extra = q_count + low // 2
+
+    def leave(start, stop):
+        at = slice(start, stop)
+        copies.extend(send([(out.at[:, at], out_hbm.at[:, at])], sems, len(copies)))
 
     def give(value, start):
         tiles = value.shape[0] // first
@@ -238,28 +251,75 @@
                     out[r * groups + g, start + q] = value[
                         at : at + SUB, g * LANE : (g + 1) * LANE
                     ]
-        at = slice(start, start + tiles)
-        copies.extend(send([(out.at[:, at], out_hbm.at[:, at])], sems, len(copies)))
-
-    give(dot3((qh[...], ql[...]), (cch[...], ccl[...])), q_count)
+        leave(start, start + tiles)
+
+    def halo_columns(value, start, held):
+        tiles = value.shape[0] // first
+        for r in range(rows):
+            for g in range(groups):
+                total = held[r, g]
+                left = max(g - 1, 0) * LANE
+                right = min(g + 1, groups - 1) * LANE
+                for q in range(tiles):
+                    at = slice(q * first + r * SUB, q * first + (r + 1) * SUB)
+                    both = jnp.where(
+                        lane < LANE // 2,
+                        value[at, right : right + LANE],
+                        value[at, left : left + LANE],
+                    )
+                    to = HALO * (start + q)
+                    both = pltpu.roll(both, (to + 2) % LANE, 1)
+                    total = jnp.where((lane >= to) & (lane < to + HALO), both, total)
+                held[r, g] = total
+
+    def coarse_columns(value, held):
+        half_lane = LANE // 2
+        for j in range(low):
+            for r in range(rows):
+                at = slice(j // 2 * first + r * SUB, j // 2 * first + (r + 1) * SUB)
+                shift = HALO * j + 2 - j % 2 * half_lane
+                to = half_lane + HALO * j
+                for g in range(groups):
+                    left = max(g - 1, 0) * LANE
+                    right = min(g + 1, groups - 1) * LANE
+                    left = pltpu.roll(value[at, left : left + LANE], shift % LANE, 1)
+                    right = pltpu.roll(
+                        value[at, right : right + LANE], (shift + half_lane) % LANE, 1
+                    )
+                    total = jnp.where((lane >= to) & (lane < to + 2), left, held[r, g])
+                    held[r, g] = jnp.where(
+                        (lane >= to + 2) & (lane < to + HALO), right, total
+                    )
+
+    columns = {
+        (r, g): jnp.zeros((SUB, LANE), jnp.float32) for r in range(rows) for g in range(groups)
+    }
+    coarse = dot3((qh[...], ql[...]), (cch[...], ccl[...]))
+    give(coarse, q_count)
+    coarse_columns(coarse, columns)
     for top in range(0, q_count * first, wide):
         at = slice(top, top + wide)
         even, odd = (
             dot3((oh[parity, at, :], ol[parity, at, :]), (ch[parity], cl[parity]))
             for parity in range(2)
         )
-        give(jnp.concatenate([even + odd, even - odd], axis=1), top // first)
+        value = jnp.concatenate([even + odd, even - odd], axis=1)
+        give(value, top // first)
+        halo_columns(value, top // first, columns)
+    for (r, g), total in columns.items():
+        out[r * groups + g, extra] = total
+    leave(extra, extra + 1)
     for copy in copies:
         copy.wait()
 
 
 def back_kernel(sizes, b, *rest):
-    (devices, q_count, tiles, planes, length) = sizes
-    away, outs, near, (lh, ll, mh, ml, sems) = rest[:4], rest[4:8], rest[8:12], rest[12:]
-    out, coarse, lo, hi = outs
+    (devices, q_count, low, tiles, planes, length) = sizes
+    away, outs, near, (lh, ll, mh, ml, sems) = rest[:8], rest[8:13], rest[13:21], rest[21:]
+    out, coarse, lo, hi, side = outs
     copies = load(list(zip(away, near)), sems)
-    eh, el, ceh, cel = near
-    cells = LANE
+    eh, el, ceh, cel, wh, wl, cwh, cwl = near
+    cells, short = LANE, length // 2
     for n in range(planes):
         for parity in range(2):
             rows = jnp.concatenate(
@@ -271,7 +331,7 @@
             )
             at = slice(n * LANE, (n + 1) * LANE)
             lh[parity, at, :], ll[parity, at, :] = split(jnp.transpose(rows))
-    halves = tiles - q_count
+    halves = low // 2
     coarse_planes = planes // 2
     for n in range(coarse_planes):
         rows = jnp.concatenate(
@@ -282,10 +342,10 @@
             ],
             axis=0,
         )
-        high, rest_part = split(jnp.transpose(rows))
-        mh[n * LANE : (n + 1) * LANE, :] = high
-        ml[n * LANE : (n + 1) * LANE, :] = rest_part
-    for copy in copies:
+        at = slice(n * LANE, (n + 1) * LANE)
+        mh[at, :], ml[at, :] = split(jnp.transpose(rows))
+
+    for copy in copies[:4]:
         copy.wait()
     for p in range(0, planes, 2):
         at = slice(p * cells, (p + 2) * cells)
@@ -300,7 +360,7 @@
             hi[: 2 * cells, :] = value
         out[at, :] = value
     value = dot3((mh[...], ml[...]), (ceh[...], cel[...]))
-    half, fourth, short = cells // 2, cells // 4, length // 2
+    half, fourth = cells // 2, cells // 4
     for n in range(coarse_planes):
         top = n * cells
         part = value[top : top + half, :short] + value[top + half : top + cells, short:]
@@ -311,6 +371,61 @@
                 top = 2 * cells + (n - start) * fourth
                 edge[top : top + fourth, :short] = part[:fourth]
                 edge[top : top + fourth, short:] = part[fourth:]
+
+    lane = lax.broadcasted_iota(jnp.int32, (SUB, LANE), 1)
+    tile = lambda s: b[(s * tiles + tiles - 1) * SUB : (s + 1) * tiles * SUB, :]
+
+    def spread(parts):
+        return jnp.concatenate(
+            [
+                jnp.concatenate(
+                    [jnp.where(lane % HALO == h, part, 0.0) for part in parts], axis=1
+                )
+                for h in range(HALO)
+            ],
+            axis=0,
+        )
+
+    for copy in copies[4:]:
+        copy.wait()
+    half_lane = LANE // 2
+    results = []
+    for parity in range(2):
+        parts = [
+            jnp.where(lane < half_lane, tile(s), pltpu.roll(tile(s + 2), half_lane, 1))
+            for s in range(parity, devices, 4)
+        ]
+        results.append(dot3(split(spread(parts)), (wh[parity], wl[parity])))
+    even, odd = results
+    value = jnp.exp(jnp.concatenate([even + odd, even - odd], axis=1))
+    side[: HALO * planes, :] = value
+    width = HALO * low
+    fit = LANE // width
+    parts = []
+    for s in range(0, devices, fit):
+        part = jnp.zeros((SUB, LANE), jnp.float32)
+        for i in range(fit):
+            moved = pltpu.roll(tile(s + i), (i * width - half_lane) % LANE, 1)
+            part = jnp.where((lane >= i * width) & (lane < (i + 1) * width), moved, part)
+        parts.append(part)
+    whole = dot3(split(spread(parts)), (cwh[...], cwl[...]))
+    side[HALO * planes :, short:] = jnp.zeros((HALO * coarse_planes, short), jnp.float32)
+    after = 2 * cells + 2 * fourth
+    for h in range(HALO):
+        top = h * SUB
+        part = whole[top : top + coarse_planes, :short] + whole[top + coarse_planes : top + SUB, short:]
+        part = jnp.exp(part)
+        at = HALO * planes + h * coarse_planes
+        side[at : at + coarse_planes, :short] = part
+        for edge, fine_at, coarse_at in ((lo, 0, 0), (hi, planes - 2, coarse_planes - 2)):
+            for i in range(2):
+                at = h * planes + fine_at + i
+                to = after + i * HALO + h
+                edge[to : to + 1, :] = value[at : at + 1, :]
+                to += 2 * HALO
+                at = coarse_at + i
+                edge[to : to + 1, :short] = part[at : at + 1, :]
+                edge[to : to + 1, short:] = jnp.zeros((1, short), jnp.float32)
 
 
 def source_kernel(planes, pairs, x, out, lo, hi, left, right, held, summed):
@@ -341,33 +456,6 @@
             edge[SUB + n : SUB + n + 1, : length // 2] = out[at : at + 1, :]
 
 
-def edge_kernel(kappa, coarse, k_lo, k_hi, first, last):
-    planes, cells, _ = kappa.shape
-    coarse_planes, half, short = coarse.shape
-    fourth = half // 2
-    for n in range(planes + 2):
-        if n == 0:
-            held = k_lo.at[cells : 2 * cells, :]
-        elif n == planes + 1:
-            held = k_hi.at[:cells, :]
-        else:
-            held = kappa.at[n - 1]
-        first[n] = held[:2, :]
-        last[n] = held[cells - 2 :, :]
-    for n in range(coarse_planes + 2):
-        at = planes + 2 + n
-        if 0 < n < coarse_planes + 1:
-            top, bottom = coarse[n - 1, :2, :], coarse[n - 1, half - 2 :, :]
-        else:
-            held, start = (k_lo, 2 * cells + fourth) if n == 0 else (k_hi, 2 * cells)
-            top = held[start : start + 2, :short]
-            bottom = held[start + fourth - 2 : start + fourth, short:]
-        first[at, :, :short] = top
-        last[at, :, :short] = bottom
-        first[at, :, short:] = jnp.zeros((2, short), jnp.float32)
-        last[at, :, short:] = jnp.zeros((2, short), jnp.float32)
-
-
 def beside(parts, ends):
     lane = lax.broadcasted_iota(jnp.int32, parts[0].shape, 1)
     ahead = [pltpu.roll(x, 1, 1) for x in parts]
@@ -382,116 +470,232 @@
     return sums
 
 
-def stencil_kernel(
-    fine, flags, kappa, k_lo, k_hi, f_lo, f_hi, k_left, k_right, f, f_left, f_right,
-    out, ks, fs, us, ws, rs, sems,
+def first_sweep(ks, fs, us, ws, rs, k_at, f_at, to, ext, length):
+    lanes = [slice(at, at + LANE) for at in range(0, length, LANE)]
+    for top in range(0, ext, SUB):
+        at = slice(top, top + SUB)
+        parts = [ks[k_at, at, x] for x in lanes]
+        for k, both, x in zip(parts, beside(parts, (parts[0], parts[-1])), lanes):
+            if top == 0:
+                above = pltpu.roll(k, 1, 0)
+            else:
+                above = ks[k_at, top - 1 : top + SUB - 1, x]
+            if top == ext - SUB:
+                below = pltpu.roll(k, SUB - 1, 0)
+            else:
+                below = ks[k_at, top + 1 : top + SUB + 1, x]
+            total = (ks[k_at - 1, at, x] + ks[k_at + 1, at, x]) + (above + below) + both
+            scale = JACOBI_WEIGHT / (6.0 * k + total)
+            u = fs[f_at, at, x] * (2.0 * scale)
+            us[to, at, x] = u
+            ws[to, at, x] = k * u
+            rs[to, at, x] = scale
+
+
+def second_sweep(ks, us, ws, rs, k_at, u_at, out, to, ext, length):
+    lanes = [slice(at, at + LANE) for at in range(0, length, LANE)]
+    for top in range(SUB, ext - SUB, SUB):
+        at = slice(top, top + SUB)
+        sums = []
+        for held in (us, ws):
+            parts = [held[u_at, at, x] for x in lanes]
+            sums.append(
+                [
+                    both
+                    + (held[u_at - 1, at, x] + held[u_at + 1, at, x])
+                    + (
+                        held[u_at, top - 1 : top + SUB - 1, x]
+                        + held[u_at, top + 1 : top + SUB + 1, x]
+                    )
+                    for both, x in zip(beside(parts, (0.0, 0.0)), lanes)
+                ]
+            )
+        for i, x in enumerate(lanes):
+            coupled = ks[k_at, at, x] * sums[0][i] + sums[1][i]
+            out[to, top - SUB : top, x] = (2.0 - JACOBI_WEIGHT) * us[u_at, at, x] + rs[
+                u_at, at, x
+            ] * coupled
+
+
+def fill_sides(flags, ks, at):
+    end = ks.shape[1] - SUB
+
+    @pl.when(flags[2] == 1)
+    def _():
+        for p in at:
+            ks[p, SUB - 1 : SUB, :] = ks[p, SUB : SUB + 1, :]
+
+    @pl.when(flags[3] == 1)
+    def _():
+        for p in at:
+            ks[p, end : end + 1, :] = ks[p, end - 1 : end, :]
+
+
+def put_source(fs, to, plane, left, right, row, length):
+    end = fs.shape[1] - SUB
+    fs[to, SUB:end, :] = plane.astype(jnp.float32)
+    fs[to, SUB - 1 : SUB, :] = left[row : row + 1, :length]
+    fs[to, end : end + 1, :] = right[row : row + 1, :length]
+
+
+def inner_level(fine, flags, kappa, side, f, f_left, f_right, out_hbm, keep_hbm, scratch):
+    ks, fs, us, ws, rs, out, sems = scratch
+    planes, cells, length = kappa.shape
+    ext, end = cells + 2 * SUB, cells + SUB
+    row = 0 if fine else HALO * 2 * planes
+    source_row = 0 if fine else SUB
+    for p in range(planes):
+        ks[p, SUB:end, :] = kappa[p]
+        for h, to in enumerate((SUB - 2, SUB - 1, end, end + 1)):
+            at = row + h * planes + p
+            ks[p, to : to + 1, :] = side[at : at + 1, :length]
+    fill_sides(flags, ks, range(planes))
+    for p in range(1, planes - 1):
+        put_source(fs, p, f[p], f_left, f_right, source_row + p, length)
+
+    def first(p, carry):
+        first_sweep(ks, fs, us, ws, rs, p, p, p, ext, length)
+        return carry
+
+    lax.fori_loop(1, planes - 1, first, 0)
+    pairs = []
+    for group, at in enumerate((1, planes - 3)):
+        pairs.append((us.at[at : at + 2], keep_hbm.at[5 * group : 5 * group + 2]))
+        pairs.append((ws.at[at : at + 2], keep_hbm.at[5 * group + 2 : 5 * group + 4]))
+        own = 1 if group == 0 else planes - 2
+        pairs.append((rs.at[own], keep_hbm.at[5 * group + 4]))
+    copies = send(pairs, sems, 0)
+    if planes > 4:
+
+        def second(p, carry):
+            second_sweep(ks, us, ws, rs, p, p, out, p, ext, length)
+            return carry
+
+        lax.fori_loop(2, planes - 2, second, 0)
+        at = slice(2, planes - 2)
+        copies += send([(out.at[at], out_hbm.at[at])], sems, len(copies))
+    return copies
+
+
+def inner_kernel(
+    flags, kappa, coarse, side, f, cf, f_left, f_right, out_hbm, keep_hbm, ckeep_hbm, *scratch
 ):
-    planes, cells, length = out.shape
-    end = SUB + cells
-    pairs = [(kappa, ks.at[2 : planes + 2, SUB:end, :])]
-
-    def place(edge, row, held, plane):
-        if fine:
-            pairs.append((edge.at[row : row + cells, :], held.at[plane, SUB:end, :]))
-            return
-        half = cells // 2
-        for h in range(2):
-            at = SUB + h * half
-            pairs.append(
-                (
-                    edge.at[row : row + half, h * length : (h + 1) * length],
-                    held.at[plane, at : at + half, :],
-                )
-            )
-
-    for i in range(2):
-        row = i * cells if fine else 4 * cells + i * cells // 2
-        place(k_lo, row, ks, i)
-        place(k_hi, row, ks, planes + 2 + i)
-    row = 0 if fine else 2 * cells
-    place(f_lo, row, fs, 0)
-    place(f_hi, row, fs, planes + 1)
-    copies = load(pairs, sems)
-    at = 0 if fine else SUB
-    for p in range(planes):
-        fs[p + 1, SUB:end, :] = f[p].astype(jnp.float32)
-        fs[p + 1, SUB - 1 : SUB, :] = f_left[at + p : at + p + 1, :length]
-        fs[p + 1, end : end + 1, :] = f_right[at + p : at + p + 1, :length]
-    at = 0 if fine else 2 * planes + 2
-    for p in range(planes + 2):
-        ks[p + 1, SUB - 2 : SUB, :] = k_left[at + p, :, :length]
-        ks[p + 1, end : end + 2, :] = k_right[at + p, :, :length]
+    half = len(scratch) // 2
+    copies = inner_level(
+        True, flags, kappa, side, f, f_left, f_right, out_hbm, keep_hbm, scratch[:half]
+    )
+    copies += inner_level(
+        False, flags, coarse, side, cf, f_left, f_right, None, ckeep_hbm, scratch[half:]
+    )
     for copy in copies:
         copy.wait()
 
-    @pl.when(flags[0] == 1)
-    def _():
-        ks[1] = ks[2]
-
-    @pl.when(flags[1] == 1)
-    def _():
-        ks[planes + 2] = ks[planes + 1]
-
-    @pl.when(flags[2] == 1)
-    def _():
-        for p in range(planes + 4):
-            ks[p, SUB - 1 : SUB, :] = ks[p, SUB : SUB + 1, :]
-
-    @pl.when(flags[3] == 1)
-    def _():
-        for p in range(planes + 4):
-            ks[p, end : end + 1, :] = ks[p, end - 1 : end, :]
-
-    lanes = [slice(at, at + LANE) for at in range(0, length, LANE)]
-
-    def first(p, carry):
-        for top in range(0, cells + 2 * SUB, SUB):
-            at = slice(top, top + SUB)
-            parts = [ks[p + 1, at, x] for x in lanes]
-            for k, both, x in zip(parts, beside(parts, (parts[0], parts[-1])), lanes):
-                if top == 0:
-                    above = pltpu.roll(k, 1, 0)
-                else:
-                    above = ks[p + 1, top - 1 : top + SUB - 1, x]
-                if top == cells + SUB:
-                    below = pltpu.roll(k, SUB - 1, 0)
-                else:
-                    below = ks[p + 1, top + 1 : top + SUB + 1, x]
-                total = (ks[p, at, x] + ks[p + 2, at, x]) + (above + below) + both
-                scale = JACOBI_WEIGHT / (6.0 * k + total)
-                u = fs[p, at, x] * (2.0 * scale)
-                us[p, at, x] = u
-                ws[p, at, x] = k * u
-                rs[p, at, x] = scale
-        return carry
-
-    lax.fori_loop(0, planes + 2, first, 0)
-
-    def second(p, carry):
-        for top in range(SUB, end, SUB):
-            at = slice(top, top + SUB)
-            sums = []
-            for held in (us, ws):
-                parts = [held[p + 1, at, x] for x in lanes]
-                sums.append(
-                    [
-                        both
-                        + (held[p, at, x] + held[p + 2, at, x])
-                        + (
-                            held[p + 1, top - 1 : top + SUB - 1, x]
-                            + held[p + 1, top + 1 : top + SUB + 1, x]
-                        )
-                        for both, x in zip(beside(parts, (0.0, 0.0)), lanes)
+
+def outer_level(
+    fine, flags, kappa, f, keep_hbm, k_edges, f_edges, f_left, f_right, out_hbm, scratch
+):
+    ks, fs, us, ws, rs, out, sems = scratch
+    planes, cells, length = kappa.shape
+    ext, end = cells + 2 * SUB, cells + SUB
+    half = cells // 2
+    fine_cells = cells if fine else 2 * cells
+    pairs = []
+    for group in range(2):
+        at, to = 5 * group, 4 * group + 2 * (1 - group)
+        pairs.append((keep_hbm.at[at : at + 2], us.at[to : to + 2]))
+        pairs.append((keep_hbm.at[at + 2 : at + 4], ws.at[to : to + 2]))
+        pairs.append((keep_hbm.at[at + 4], rs.at[2 if group == 0 else 5]))
+    copies = load(pairs, sems)
+
+    def place(held, to, edge, row):
+        if fine:
+            held[to, SUB:end, :] = edge[row : row + cells, :]
+        else:
+            held[to, SUB : SUB + half, :] = edge[row : row + half, :length]
+            held[to, SUB + half : end, :] = edge[row : row + half, length:]
+
+    after = 2 * fine_cells + fine_cells // 2 + (0 if fine else 2 * HALO)
+    for group, edge in enumerate(k_edges):
+        for i in range(2):
+            row = i * cells if fine else 2 * fine_cells + i * half
+            to = 4 * group + 2 * group + i
+            place(ks, to, edge, row)
+            for h, at in enumerate((SUB - 2, SUB - 1, end, end + 1)):
+                row = after + i * HALO + h
+                ks[to, at : at + 1, :] = edge[row : row + 1, :length]
+            ks[4 * group + 2 * (1 - group) + i, SUB:end, :] = kappa[
+                i if group == 0 else planes - 2 + i
+            ]
+    source_row = 0 if fine else SUB
+    for group, edge in enumerate(f_edges):
+        place(fs, 3 * group, edge, 0 if fine else fine_cells)
+        own = 0 if group == 0 else planes - 1
+        put_source(fs, 1 + group, f[own], f_left, f_right, source_row + own, length)
+    return copies
+
+
+def outer_kernel(flags, kappa, coarse, side, f, cf, keep, ckeep, *rest):
+    (k_lo, k_hi, f_lo, f_hi, f_left, f_right, _, out, cout), scratch = rest[:9], rest[9:]
+    half = len(scratch) // 2
+    levels = []
+    for fine in (True, False):
+        held = scratch[:half] if fine else scratch[half:]
+        own, source, kept = (kappa, f, keep) if fine else (coarse, cf, ckeep)
+        copies = outer_level(
+            fine, flags, own, source, kept, (k_lo, k_hi), (f_lo, f_hi), f_left, f_right, None, held
+        )
+        levels.append((fine, own, held, copies, out if fine else cout))
+    sent = []
+    for fine, own, (ks, fs, us, ws, rs, done, sems), copies, target in levels:
+        planes, cells, length = own.shape
+        ext, end = cells + 2 * SUB, cells + SUB
+        row = 0 if fine else HALO * 2 * planes
+        for group in range(2):
+            for i in range(2):
+                p = i if group == 0 else planes - 2 + i
+                to = 4 * group + 2 * (1 - group) + i
+                for h, at in enumerate((SUB - 2, SUB - 1, end, end + 1)):
+                    ks[to, at : at + 1, :] = side[
+                        row + h * planes + p : row + h * planes + p + 1, :length
                     ]
-                )
-            for i, x in enumerate(lanes):
-                coupled = ks[p + 2, at, x] * sums[0][i] + sums[1][i]
-                out[p, top - SUB : top, x] = (2.0 - JACOBI_WEIGHT) * us[
-                    p + 1, at, x
-                ] + rs[p + 1, at, x] * coupled
-        return carry
-
-    lax.fori_loop(0, planes, second, 0)
+
+        @pl.when(flags[0] == 1)
+        def _():
+            ks[1] = ks[2]
+
+        @pl.when(flags[1] == 1)
+        def _():
+            ks[6] = ks[5]
+
+        fill_sides(flags, ks, range(8))
+
+        def first(i, carry):
+            k_at = jnp.where(i < 2, i + 1, i + 3)
+            to = jnp.where(i < 2, i, i + 4)
+            first_sweep(ks, fs, us, ws, rs, k_at, i, to, ext, length)
+            return carry
+
+        lax.fori_loop(0, 4, first, 0)
+        for copy in copies:
+            copy.wait()
+
+        def second(i, carry):
+            second_sweep(
+                ks, us, ws, rs, i + 2, jnp.where(i < 2, i + 1, i + 3), done, i, ext, length
+            )
+            return carry
+
+        lax.fori_loop(0, 4, second, 0)
+        sent += send(
+            [
+                (done.at[0:2], target.at[0:2]),
+                (done.at[2:4], target.at[planes - 2 : planes]),
+            ],
+            sems,
+            6,
+        )
+    for copy in sent:
+        copy.wait()
 
 
 SMEM = pl.BlockSpec(memory_space=pltpu.SMEM)
@@ -500,7 +704,7 @@
 ANY = pl.BlockSpec(memory_space=pl.ANY)
 
 
-def call(kernel, outs, operands, scratch, flops, specs, limit):
+def call(kernel, outs, operands, scratch, flops, specs, limit, out_specs=None, aliases=None):
     many = isinstance(outs, (list, tuple))
     written = outs if many else [outs]
     moved = sum(math.prod(x.shape) * x.dtype.itemsize for x in (*operands, *written))
@@ -508,13 +712,16 @@
         pltpu.with_memory_space_constraint(x, pltpu.HBM) if spec is AWAY else x
         for x, spec in zip(operands, specs)
     ]
-    out_specs = [VMEM if isinstance(x, jax.ShapeDtypeStruct) else AWAY for x in written]
+    out_specs = out_specs or [
+        VMEM if isinstance(x, jax.ShapeDtypeStruct) else AWAY for x in written
+    ]
     return pl.pallas_call(
         kernel,
         out_shape=outs,
         in_specs=specs,
         out_specs=out_specs if many else out_specs[0],
         scratch_shapes=scratch,
+        input_output_aliases=aliases or {},
         compiler_params=pltpu.CompilerParams(vmem_limit_bytes=limit * MIB),
         cost_estimate=pl.CostEstimate(flops=flops, bytes_accessed=moved, transcendentals=0),
     )(*operands)
@@ -538,25 +745,18 @@
     return lax.ppermute(hi, axis, up), lax.ppermute(lo, axis, down)
 
 
-def smooth(fine, flags, kappa, halo, source, edges):
-    planes, cells, length = source.shape
-    k_lo, k_hi, k_left, k_right = halo
-    f_lo, f_hi, f_left, f_right = edges
-    ext = cells + 2 * SUB
-    wide = pltpu.VMEM((planes + 2, ext, length), jnp.float32)
-    return call(
-        functools.partial(stencil_kernel, fine),
-        f32(planes, cells, length),
-        (flags, kappa, k_lo, k_hi, f_lo, f_hi, k_left, k_right, source, f_left, f_right),
-        [
-            pltpu.VMEM((planes + 4, ext, length), jnp.float32),
-            wide, wide, wide, wide,
-            pltpu.SemaphoreType.DMA((13,)),
-        ],
-        60 * kappa.size,
-        [SMEM] + [ANY] * 5 + [VMEM] * 5,
-        32,
-    )
+def level_scratch(shape, k_planes, f_planes, out_planes):
+    planes, cells, length = shape
+    wide = lambda n: pltpu.VMEM((n, cells + 2 * SUB, length), jnp.float32)
+    return [
+        wide(k_planes),
+        wide(f_planes),
+        wide(k_planes),
+        wide(k_planes),
+        wide(k_planes),
+        pltpu.VMEM((out_planes, cells, length), jnp.float32),
+        pltpu.SemaphoreType.DMA((8,)),
+    ]
 
 
 def fused_body(noise, source):
@@ -624,7 +824,7 @@
         + two_parts(inverse_first_coarse(first // 2, rows))
         + two_parts(second_coarse(second // 2, groups))
     )
-    tiles = 2 * held + low // 2
+    tiles = 2 * held + low // 2 + 1
     modes = (me + devices * np.array(js)).astype(jnp.float32)
     weight = jnp.where(modes == 0.0, norm, 2.0 * norm).astype(jnp.float32)
     scale = jnp.stack([DECAY * modes * modes, weight], axis=1)
@@ -652,32 +852,54 @@
     )
     got = lax.all_to_all(out, EVERY, split_axis=0, concat_axis=0, tiled=True)
 
-    constants = two_parts(inverse_third(length, devices, js)) + two_parts(
-        third_coarse(length // 2, devices, js[:low])
-    )
-    edge = f32(2 * cells + cells // 2, length)
-    fine, coarse, lo, hi = call(
-        functools.partial(back_kernel, (devices, 2 * held, tiles, planes, length)),
-        [f32(*flat), f32(planes * cells // 4, length // 2), edge, edge],
+    third = inverse_third(length, devices, js)
+    constants = (
+        two_parts(third)
+        + two_parts(third_coarse(length // 2, devices, js[:low]))
+        + two_parts(np.repeat(third, HALO, axis=1))
+        + two_parts(third_coarse_halo(length // 2, devices, js[:low]))
+    )
+    edge = f32(2 * cells + cells // 2 + 4 * HALO, length)
+    side = f32(HALO * planes * 3 // 2, length)
+    fine, coarse, lo, hi, side = call(
+        functools.partial(back_kernel, (devices, 2 * held, low, tiles, planes, length)),
+        [f32(*flat), f32(planes * cells // 4, length // 2), edge, edge, side],
         (got.reshape(devices * tiles * SUB, LANE), *constants),
         room(*constants)
         + [pltpu.VMEM((2, planes * cells, devices * held), bf16)] * 2
         + [pltpu.VMEM((planes // 2 * LANE, devices * low), bf16)] * 2
-        + [pltpu.SemaphoreType.DMA((4,))],
+        + [pltpu.SemaphoreType.DMA((8,))],
         6 * planes * cells * length * length,
-        [VMEM] + [AWAY] * 4,
-        24,
+        [VMEM] + [AWAY] * 8,
+        28,
     )
     fine, coarse = fine.reshape(source.shape), coarse.reshape(coarse_source.shape)
     k_lo, k_hi = swap(lo, hi, "row")
-    side = f32(planes + planes // 2 + 4, 2, length)
-    left, right = call(
-        edge_kernel, [side, side], (fine, coarse, k_lo, k_hi), [], fine.size, [VMEM] * 4, 16
-    )
-    halo = (k_lo, k_hi, *swap(left, right, PLANE))
-    fine_pressure = smooth(True, flags, fine, halo, source, edges)
-    coarse_pressure = smooth(False, flags, coarse, halo, coarse_source, edges)
-    return fine_pressure, coarse_pressure
+    f_lo, f_hi, f_left, f_right = edges
+    kept = lambda x: jax.ShapeDtypeStruct((10, x.shape[1] + 2 * SUB, x.shape[2]), jnp.float32)
+    own = (flags, fine, coarse, side, source, coarse_source)
+    inner, keep, coarse_keep = call(
+        inner_kernel,
+        [pltpu.HBM(fine.shape, jnp.float32), kept(fine), kept(coarse)],
+        (*own, f_left, f_right),
+        level_scratch(fine.shape, planes, planes, planes)
+        + level_scratch(coarse.shape, planes // 2, planes // 2, planes // 2),
+        30 * fine.size,
+        [SMEM] + [VMEM] * 7,
+        32,
+        [AWAY, ANY, ANY],
+    )
+    return call(
+        outer_kernel,
+        [pltpu.HBM(fine.shape, jnp.float32), pltpu.HBM(coarse.shape, jnp.float32)],
+        (*own, keep, coarse_keep, k_lo, k_hi, f_lo, f_hi, f_left, f_right, inner),
+        level_scratch(fine.shape, 8, 4, 4) + level_scratch(coarse.shape, 8, 4, 4),
+        30 * fine.size,
+        [SMEM] + [VMEM] * 5 + [ANY] * 2 + [VMEM] * 6 + [AWAY],
+        32,
+        [AWAY] * 2,
+        {14: 0},
+    )
 
 
 NEIGHBOUR_STEPS = ((1, 0, 0), (-1, 0, 0), (0, 1, 0), (0, -1, 0), (0, 0, 1), (0, 0, -1))

time: 171 us -> 165 us (0.965)
  waiting for transfers between devices: 49.9 us -> 39 us
  Pallas kernels: 30 us -> 34.1 us
  starting transfers between devices: 25.5 us -> 22.5 us
  blocking collectives: 61.9 us -> 64.6 us
    ppermute x8 -> x6, waiting for transfers between devices: 39.9 us -> 29 us  [swap(): return (lax.ppermute(hi, axis, up), lax.ppermute(lo, axis, down))]
    pallas_call x7 -> x6, Pallas kernels: 30 us -> 34.1 us  [call(): pl.pallas_call(kernel, out_shape=outs, in_specs=specs, out_specs=out_spec...]
    ppermute x8 -> x6, starting transfers between devices: 18.4 us -> 15.4 us  [swap(): return (lax.ppermute(hi, axis, up), lax.ppermute(lo, axis, down))]
    all_to_all x1, blocking collectives: 61.9 us -> 64.6 us  [fused_body(): got = lax.all_to_all(out, EVERY, split_axis=0, concat_axis=0, tiled=True)]
  transfers between devices with their start and end apart: 9 -> 7, of which waited for: 6 -> 5; matrix products, arithmetic and copies ran while one was open for 0% -> 0% of each run, Pallas kernels for 1% -> 4%
where the time goes in v1:
time: 165 us; the launch traced here: 164 us
  blocking collectives  64.6 us (39%)
  waiting for transfers between devices  39 us (24%)
  Pallas kernels  34.1 us (21%)
  starting transfers between devices  22.5 us (14%)
  local copies, waits for them, and re-layouts  3.44 us (2%)
    all_to_all x1, blocking collectives, fused_body(): got = lax.all_to_all(out, EVERY, split_axis=0, concat_axis=0, tiled=True)  64.6 us
    pallas_call x6, Pallas kernels, call(): pl.pallas_call(kernel, out_shape=outs, in_specs=specs, out_specs=out_spec...  34.1 us
    ppermute x6, waiting for transfers between devices, swap(): return (lax.ppermute(hi, axis, up), lax.ppermute(lo, axis, down))  29 us
    ppermute x6, starting transfers between devices, swap(): return (lax.ppermute(hi, axis, up), lax.ppermute(lo, axis, down))  15.4 us
    all_to_all x1, waiting for transfers between devices, fused_body(): lax.all_to_all(sent, EVERY, split_axis=0, concat_axis=0, tiled=True)  9.98 us
    all_to_all x1, starting transfers between devices, fused_body(): lax.all_to_all(sent, EVERY, split_axis=0, concat_axis=0, tiled=True)  7.1 us
    unnamed x12, local copies, waits for them, and re-layouts  3.36 us
  transfers between devices with their start and end apart: 7, of which 5 were waited for; matrix products, arithmetic and copies ran while one was open for 0% of the time, Pallas kernels for 4%

profile of v1, /device:TPU:1, one launch (start us, length us, event | category | flops | bytes accessed | tf_op | source)
XLA Modules:
  0.0 164.5 jit_solution(345819786923492359)
XLA Ops:
  0.6 5.5 %shard_map.248 = f32[4096,128]{1,0:T(8,128)} custom-call(bf16[1024,512]{1,0:T(8,128)(2,1)} %constant.77.clone.d_hbm, bf16[1024,512]{1,0:T(8,128)(2,1)} %bitcast.24), custom_call_target="tpu_custom_call" | custom-call | flops 1073741824 | bytes 4194304 | tf_op jit(solution)/shard_map/pallas_call | solution.py:718
  6.2 7.1 %all-to-all-start = ((f32[32,16,8,128]{3,2,1,0:T(8,128)}), f32[32,16,8,128]{3,2,1,0:T(8,128)S(1)}, u32[]{:S(2)}, u32[]{:S(2)}) async-start(f32[32,16,8,128]{3,2,1,0:T(8,128)} %bitcast.23), calls=%async_computation | async-start | bytes 4194304 | tf_op jit(solution)/shard_map/all_to_all | solution.py:797
  13.3 0.9 copy-done.3
  14.2 1.3 shard_map.249
  15.5 3.5 %collective-permute-start = (f32[160,512]{1,0:T(8,128)}, f32[160,512]{1,0:T(8,128)}, u32[]{:S(2)}, u32[]{:S(2)}) collective-permute-start(f32[160,512]{1,0:T(8,128)} %get-tuple-element.25), channel_id=1, source_target_pairs={{0,2},{2,4},{4,6},{6,8},{8,10},{10,12},{12,14},{1,3},{3,5},{5,7},{... | collective-permute-start | bytes 983048 | tf_op jit(solution)/shard_map/ppermute | solution.py:745
  19.0 1.9 %collective-permute-start.1 = (f32[160,512]{1,0:T(8,128)}, f32[160,512]{1,0:T(8,128)}, u32[]{:S(2)}, u32[]{:S(2)}) collective-permute-start(f32[160,512]{1,0:T(8,128)} %get-tuple-element.26), channel_id=1, source_target_pairs={{2,0},{4,2},{6,4},{8,6},{10,8},{12,10},{14,12},{3,1},{5,3},{7,5},{... | collective-permute-start | bytes 983048 | tf_op jit(solution)/shard_map/ppermute | solution.py:745
  21.0 3.1 %collective-permute-start.2 = (f32[16,512]{1,0:T(8,128)}, f32[16,512]{1,0:T(8,128)S(1)}, u32[]{:S(2)}, u32[]{:S(2)}) collective-permute-start(f32[16,512]{1,0:T(8,128)} %get-tuple-element.27), channel_id=1, source_target_pairs={{0,1},{1,16},{16,17},{2,3},{3,18},{18,19},{4,5},{5,20},{20,21},{6,... | collective-permute-start | bytes 98312 | tf_op jit(solution)/shard_map/ppermute | solution.py:745
  24.1 1.3 collective-permute-start.3
  25.4 0.1 copy.30.scale
  25.5 3.0 %collective-permute-done.2.f_left.rest_4_ = f32[16,512]{1,0:T(8,128)S(1)} collective-permute-done((f32[16,512]{1,0:T(8,128)}, f32[16,512]{1,0:T(8,128)S(1)}, u32[]{:S(2)}, u32[]{:S(2)}) %collective-permute-start.2) | collective-permute-done | bytes 32800 | tf_op jit(solution)/shard_map/ppermute | solution.py:745
  28.5 2.1 %collective-permute-done.3.f_right.rest_5_ = f32[16,512]{1,0:T(8,128)S(1)} collective-permute-done((f32[16,512]{1,0:T(8,128)S(1)}, f32[16,512]{1,0:T(8,128)S(1)}, u32[]{:S(2)}, u32[]{:S(2)}) %collective-permute-start.3) | collective-permute-done | bytes 32800 | tf_op jit(solution)/shard_map/ppermute | solution.py:745
  30.6 20.8 %collective-permute-done.rest_2_ = f32[160,512]{1,0:T(8,128)} collective-permute-done((f32[160,512]{1,0:T(8,128)}, f32[160,512]{1,0:T(8,128)}, u32[]{:S(2)}, u32[]{:S(2)}) %collective-permute-start) | collective-permute-done | bytes 327712 | tf_op jit(solution)/shard_map/ppermute | solution.py:745
  51.4 10.0 %all-to-all-done.b = f32[32,16,8,128]{3,2,1,0:T(8,128)S(1)} async-done(((f32[32,16,8,128]{3,2,1,0:T(8,128)}), f32[32,16,8,128]{3,2,1,0:T(8,128)S(1)}, u32[]{:S(2)}, u32[]{:S(2)}) %all-to-all-start) | async-done | bytes 2097184 | tf_op jit(solution)/shard_map/all_to_all | solution.py:797
  61.4 8.5 %shard_map.250 = f32[32,19,8,128]{3,2,1,0:T(8,128)} custom-call(f32[8,2]{1,0:T(8,128)S(1)} %copy.30.scale, f32[32,16,8,128]{3,2,1,0:T(8,128)S(1)} %all-to-all-done.b, bf16[2,256,256]{2,1,0:T(8,128)(2,1)} %constant.80.clone.rest_0_, bf16[2,256,256]{2,1,0:T(8,128)(2,1)} %constant.81.clone.rest_1_, bf16[128,128]{1,0:T(8,128)(2,1)} %constant.82.clone.rest_2_, ...), custom_call_target="tpu_custom_call" | custom-call | flops 4026531840 | bytes 6848576 | tf_op jit(solution)/shard_map/pallas_call | solution.py:718
  69.9 64.6 %all_to_all.10 = f32[32,19,8,128]{3,2,1,0:T(8,128)S(1)} all-to-all(f32[32,19,8,128]{3,2,1,0:T(8,128)} %shard_map.250), channel_id=1, replica_groups=mesh['level'=2,'row'=8,'col'=2] {'row','level','col'}, dimensions={0} | all-to-all | bytes 4980736 | tf_op jit(solution)/shard_map/all_to_all | solution.py:853
  134.4 5.3 %shard_map.251 = (f32[1024,512]{1,0:T(8,128)S(1)}, f32[256,256]{1,0:T(8,128)S(1)}, f32[336,512]{1,0:T(8,128)}, f32[336,512]{1,0:T(8,128)}, f32[48,512]{1,0:T(8,128)S(1)}) custom-call(f32[4864,128]{1,0:T(8,128)S(1)} %bitcast.15, bf16[2,256,256]{2,1,0:T(8,128)(2,1)} %constant.92.clone.rest_0_, bf16[2,256,256]{2,1,0:T(8,128)(2,1)} %constant.93.clone.rest_1_, ...), custom_call_target="tpu_custom_call" | custom-call | flops 1610612736 | bytes 10256384 | tf_op jit(solution)/shard_map/pallas_call | solution.py:718
  139.8 0.7 copy-done.1
  140.5 3.6 %collective-permute-start.4 = (f32[336,512]{1,0:T(8,128)}, f32[336,512]{1,0:T(8,128)}, u32[]{:S(2)}, u32[]{:S(2)}) collective-permute-start(f32[336,512]{1,0:T(8,128)} %get-tuple-element.39), channel_id=1, source_target_pairs={{0,2},{2,4},{4,6},{6,8},{8,10},{10,12},{12,14},{1,3},{3,5},{5,7},{... | collective-permute-start | bytes 2064392 | tf_op jit(solution)/shard_map/ppermute | solution.py:745
  144.1 1.9 %collective-permute-start.5 = (f32[336,512]{1,0:T(8,128)}, f32[336,512]{1,0:T(8,128)}, u32[]{:S(2)}, u32[]{:S(2)}) collective-permute-start(f32[336,512]{1,0:T(8,128)} %get-tuple-element.40), channel_id=1, source_target_pairs={{2,0},{4,2},{6,4},{8,6},{10,8},{12,10},{14,12},{3,1},{5,3},{7,5},{... | collective-permute-start | bytes 2064392 | tf_op jit(solution)/shard_map/ppermute | solution.py:745
  146.2 0.9 copy-done.2
  147.1 0.8 copy-done.5
  147.9 5.7 %shard_map.252 = (f32[8,128,512]{2,1,0:T(8,128)}, f32[10,144,512]{2,1,0:T(8,128)S(1)}, f32[10,80,256]{2,1,0:T(8,128)S(1)}) custom-call(s32[4]{0:T(128)S(1)} %add_convert_fusion.flags, f32[8,128,512]{2,1,0:T(8,128)S(1)} %bitcast.17, f32[4,64,256]{2,1,0:T(8,128)S(1)} %bitcast.21, f32[48,512]{1,0:T(8,128)S(1)} %get-tuple-element.33.side, ...), custom_call_target="tpu_custom_call" | custom-call | flops 15728640 | bytes 9699344 | tf_op jit(solution)/shard_map/pallas_call | solution.py:718
  153.6 3.1 %collective-permute-done.5.rest_1_ = f32[336,512]{1,0:T(8,128)} collective-permute-done((f32[336,512]{1,0:T(8,128)}, f32[336,512]{1,0:T(8,128)}, u32[]{:S(2)}, u32[]{:S(2)}) %collective-permute-start.5) | collective-permute-done | bytes 688160 | tf_op jit(solution)/shard_map/ppermute | solution.py:745
  156.7 7.8 %shard_map.253 = (f32[8,128,512]{2,1,0:T(8,128)}, f32[4,64,256]{2,1,0:T(8,128)}) custom-call(s32[4]{0:T(128)S(1)} %add_convert_fusion.flags, f32[8,128,512]{2,1,0:T(8,128)S(1)} %bitcast.18, f32[4,64,256]{2,1,0:T(8,128)S(1)} %bitcast.22, f32[48,512]{1,0:T(8,128)S(1)} %get-tuple-element.33.side, ...), custom_call_target="tpu_custom_call", output_to_operand_aliasing={{0}: (14, {})} | custom-call | flops 15728640 | bytes 14090256 | tf_op jit(solution)/shard_map/pallas_call | solution.py:718
  (13 shorter events, 0.1 us)
Async XLA Ops:
  6.2 7.1 %copy-start = (bf16[8,128,512]{2,1,0:T(8,128)(2,1)S(1)}, bf16[8,128,512]{2,1,0:T(8,128)(2,1)}, u32[]{:S(2)}) copy-start(bf16[8,128,512]{2,1,0:T(8,128)(2,1)} %f.1) | copy-start | bytes 3145732
  6.2 55.2 %all-to-all-start = ((f32[32,16,8,128]{3,2,1,0:T(8,128)}), f32[32,16,8,128]{3,2,1,0:T(8,128)S(1)}, u32[]{:S(2)}, u32[]{:S(2)}) async-start(f32[32,16,8,128]{3,2,1,0:T(8,128)} %bitcast.23), calls=%async_computation | async-start | bytes 4194304 | tf_op jit(solution)/shard_map/all_to_all | solution.py:797
  13.3 1.0 copy-start.3
  15.5 35.9 %collective-permute-start = (f32[160,512]{1,0:T(8,128)}, f32[160,512]{1,0:T(8,128)}, u32[]{:S(2)}, u32[]{:S(2)}) collective-permute-start(f32[160,512]{1,0:T(8,128)} %get-tuple-element.25), channel_id=1, source_target_pairs={{0,2},{2,4},{4,6},{6,8},{8,10},{10,12},{12,14},{1,3},{3,5},{5,7},{... | collective-permute-start | bytes 983048 | tf_op jit(solution)/shard_map/ppermute | solution.py:745
  19.0 32.3 %collective-permute-start.1 = (f32[160,512]{1,0:T(8,128)}, f32[160,512]{1,0:T(8,128)}, u32[]{:S(2)}, u32[]{:S(2)}) collective-permute-start(f32[160,512]{1,0:T(8,128)} %get-tuple-element.26), channel_id=1, source_target_pairs={{2,0},{4,2},{6,4},{8,6},{10,8},{12,10},{14,12},{3,1},{5,3},{7,5},{... | collective-permute-start | bytes 983048 | tf_op jit(solution)/shard_map/ppermute | solution.py:745
  21.0 7.5 %collective-permute-start.2 = (f32[16,512]{1,0:T(8,128)}, f32[16,512]{1,0:T(8,128)S(1)}, u32[]{:S(2)}, u32[]{:S(2)}) collective-permute-start(f32[16,512]{1,0:T(8,128)} %get-tuple-element.27), channel_id=1, source_target_pairs={{0,1},{1,16},{16,17},{2,3},{3,18},{18,19},{4,5},{5,20},{20,21},{6,... | collective-permute-start | bytes 98312 | tf_op jit(solution)/shard_map/ppermute | solution.py:745
  24.1 6.5 %collective-permute-start.3 = (f32[16,512]{1,0:T(8,128)S(1)}, f32[16,512]{1,0:T(8,128)S(1)}, u32[]{:S(2)}, u32[]{:S(2)}) collective-permute-start(f32[16,512]{1,0:T(8,128)S(1)} %get-tuple-element.28), channel_id=1, source_target_pairs={{1,0},{16,1},{17,16},{3,2},{18,3},{19,18},{5,4},{20,5},{21,20},{7,... | collective-permute-start | bytes 98312 | tf_op jit(solution)/shard_map/ppermute | solution.py:745
  30.6 39.3 %copy-start.4 = (f32[16,512]{1,0:T(8,128)}, f32[16,512]{1,0:T(8,128)S(1)}, u32[]{:S(2)}) copy-start(f32[16,512]{1,0:T(8,128)S(1)} %collective-permute-done.3.f_right.rest_5_) | copy-start | bytes 98308
  139.8 0.7 copy-start.1
  140.5 13.1 %collective-permute-start.4 = (f32[336,512]{1,0:T(8,128)}, f32[336,512]{1,0:T(8,128)}, u32[]{:S(2)}, u32[]{:S(2)}) collective-permute-start(f32[336,512]{1,0:T(8,128)} %get-tuple-element.39), channel_id=1, source_target_pairs={{0,2},{2,4},{4,6},{6,8},{8,10},{10,12},{12,14},{1,3},{3,5},{5,7},{... | collective-permute-start | bytes 2064392 | tf_op jit(solution)/shard_map/ppermute | solution.py:745
  144.1 12.6 %collective-permute-start.5 = (f32[336,512]{1,0:T(8,128)}, f32[336,512]{1,0:T(8,128)}, u32[]{:S(2)}, u32[]{:S(2)}) collective-permute-start(f32[336,512]{1,0:T(8,128)} %get-tuple-element.40), channel_id=1, source_target_pairs={{2,0},{4,2},{6,4},{8,6},{10,8},{12,10},{14,12},{3,1},{5,3},{7,5},{... | collective-permute-start | bytes 2064392 | tf_op jit(solution)/shard_map/ppermute | solution.py:745
  146.2 1.0 copy-start.2
  147.1 0.8 copy-start.5
